TPU v7x, 32 devices: a whole 2x2x4 slice. The times are simulated.
32 devices in a mesh: dp: 8 (over z, y), tensor: 4 (over x, core).
Axes of the slice: x: 2, y: 2, z: 4, core: 2. Of those that a mesh axis runs over, the one named last changes fastest.
Arguments:
- tokens: bfloat16 [8192, 1152], P('dp'), may hold values from -6 to 6
- condition: bfloat16 [16, 1152], replicated, may hold values from -6 to 6
- latent_lengths: int32 [16], replicated, may hold values from 1 to 1024, as said below
- in_weight: bfloat16 [1152, 3, 1152], P(None, None, 'tensor'), may hold values from -0.1875 to 0.1875
- in_bias: bfloat16 [2, 1152], P(None, 'tensor'), may hold values from -3 to 3
- out_weight: bfloat16 [1152, 1152], P(None, 'tensor'), may hold values from -1.5 to 1.5
- out_bias: bfloat16 [1152], replicated, may hold values from -3 to 3
- up_weight: bfloat16 [1152, 4608], P(None, 'tensor'), may hold values from -0.1875 to 0.1875
- up_bias: bfloat16 [4608], P('tensor'), may hold values from -3 to 3
- down_weight: bfloat16 [1152, 4608], P(None, 'tensor'), may hold values from -0.09375 to 0.09375
- down_bias: bfloat16 [1152], replicated, may hold values from -3 to 3
- mod_weight: bfloat16 [1152, 6912], P(None, 'tensor'), may hold values from -0.1875 to 0.1875
- mod_bias: bfloat16 [6912], P('tensor'), may hold values from -3 to 3
- out_grad: bfloat16 [8192, 1152], P('dp'), may hold values from -6 to 6
Outputs:
- output: bfloat16 [8192, 1152], P(('dp', 'tensor'))
- grad_tokens: float32 [8192, 1152], P('dp', 'tensor')
- grad_condition: float32 [16, 1152], P('dp', 'tensor')
- grad_in_weight: float32 [1152, 3, 1152], P('dp', None, 'tensor')
- grad_in_bias: float32 [2, 1152], P(None, 'tensor')
- grad_out_weight: float32 [1152, 1152], P('dp', 'tensor')
- grad_out_bias: float32 [1152], replicated
- grad_up_weight: float32 [1152, 4608], P('dp', 'tensor')
- grad_up_bias: float32 [4608], P('tensor')
- grad_down_weight: float32 [1152, 4608], P('dp', 'tensor')
- grad_down_bias: float32 [1152], replicated
- grad_mod_weight: float32 [1152, 6912], P('dp', 'tensor')
- grad_mod_bias: float32 [6912], P('tensor')
Inputs may be any that keep to these rules, and one draw needn't show every extreme that they name: `latent_lengths`: lengths of the 16 latents in stream order; they sum to 8192.
All inputs are finite; a program needn't handle non-finite values.
Results may differ from a plain program's by a relative error of at most 0.017.
Values may be sent and summed in bfloat16 or wider, within the bound.
No kernel may reach another device: no remote copies, remote signals or barrier semaphores. Data moves between devices by JAX's collectives and lax.ppermute only.
A program may use at most 256 MiB of HBM per device.

v0:
```python
import jax
import jax.numpy as jnp
from jax import lax
from jax.sharding import PartitionSpec as P

HD = 72
REACH = 1


def from_behind(block, axis, distance):
    devices = range(lax.axis_size(axis))
    route = [(i - distance, i) for i in devices if i - distance in devices]
    return lax.ppermute(block, axis, route)


def layer_norm(value):
    center = value - jnp.mean(value, axis=-1, keepdims=True)
    spread = jnp.mean(center * center, axis=-1, keepdims=True)
    return center * lax.rsqrt(spread + 1e-06)


def gelu_tanh(value):
    return jax.nn.gelu(value, approximate=True)


def onehot_sum(select, values):
    upper = values.astype(jnp.bfloat16)
    lower = (values - upper.astype(jnp.float32)).astype(jnp.bfloat16)
    first = jnp.einsum("tl,tm->lm", select, upper, preferred_element_type=jnp.float32)
    return first + jnp.einsum("tl,tm->lm", select, lower, preferred_element_type=jnp.float32)


def on_device(
    tokens,
    condition,
    latent_lengths,
    in_weight,
    in_bias,
    out_weight,
    out_bias,
    up_weight,
    up_bias,
    down_weight,
    down_bias,
    mod_weight,
    mod_bias,
    out_grad,
):
    rows = tokens.shape[0]
    width = tokens.shape[1]
    latents = condition.shape[0]
    local_width = in_weight.shape[2]
    heads_here = local_width // HD
    tensor_size = lax.axis_size("tensor")
    data_size = lax.axis_size("dp")
    data_index = lax.axis_index("dp")
    factor = HD ** (-0.5)
    window = (2 * REACH + 1) * rows
    quarter = rows // tensor_size
    row_start = lax.axis_index("tensor") * quarter

    def mine(value):
        return lax.dynamic_slice_in_dim(value, row_start, quarter, 0)

    starts = jnp.cumsum(latent_lengths) - latent_lengths

    def latent_at(places):
        inside = (places >= 0) & (places < rows * data_size)
        found = jnp.sum((places[:, None] >= starts[None, :]).astype(jnp.int32), axis=1) - 1
        return jnp.where(inside, found, -2)

    first_row = data_index * rows
    own_latent = latent_at(first_row + jnp.arange(rows, dtype=jnp.int32))
    window_latent = latent_at(first_row - REACH * rows + jnp.arange(window, dtype=jnp.int32))
    matches = own_latent[:, None] == jnp.arange(latents, dtype=jnp.int32)[None, :]
    select = matches.astype(jnp.bfloat16)
    cond_full = condition.astype(jnp.float32)
    silu_cond = jax.nn.silu(cond_full).astype(jnp.bfloat16)
    mod_local = (
        jnp.dot(silu_cond, mod_weight, preferred_element_type=jnp.float32)
        + mod_bias.astype(jnp.float32)
    ).astype(jnp.bfloat16)
    modulation = lax.all_gather(mod_local, "tensor", axis=1, tiled=True)
    per_token = jnp.dot(select, modulation, preferred_element_type=jnp.float32).reshape(
        rows, 6, width
    )
    shift_a = per_token[:, 0]
    scale_a = per_token[:, 1]
    gate_a = per_token[:, 2]
    shift_m = per_token[:, 3]
    scale_m = per_token[:, 4]
    gate_m = per_token[:, 5]
    tokens_full = tokens.astype(jnp.float32)
    normed, norm_back = jax.vjp(layer_norm, tokens_full)
    entry = (normed * (1.0 + scale_a) + shift_a).astype(jnp.bfloat16)
    projected = jnp.einsum("td,dcf->ctf", entry, in_weight, preferred_element_type=jnp.float32)
    bias_full = in_bias.astype(jnp.float32)
    query = (projected[0] + bias_full[0]).astype(jnp.bfloat16)
    keys = projected[1].astype(jnp.bfloat16)
    values = (projected[2] + bias_full[1]).astype(jnp.bfloat16)
    pair = jnp.stack([keys, values])
    hops = list(range(REACH, 0, -1)) + [0] + list(range(-1, -REACH - 1, -1))
    pieces = []
    for hop in hops:
        if hop == 0:
            pieces.append(pair)
        else:
            pieces.append(from_behind(pair, "dp", hop))
    gathered = jnp.concatenate(pieces, axis=1)
    win_keys = gathered[0].reshape(window, heads_here, HD)
    win_values = gathered[1].reshape(window, heads_here, HD)
    block = min(512, rows)
    block_starts = jnp.arange(rows // block, dtype=jnp.int32) * block

    def scores_of(start):
        query_blk = lax.dynamic_slice_in_dim(query, start, block, 0).reshape(block, heads_here, HD)
        raw = (
            jnp.einsum("qhc,khc->hqk", query_blk, win_keys, preferred_element_type=jnp.float32)
            * factor
        )
        latent_blk = lax.dynamic_slice_in_dim(own_latent, start, block, 0)
        allowed = latent_blk[:, None] == window_latent[None, :]
        return (jnp.where(allowed[None], raw, -1e30), query_blk)

    def forward_block(start):
        scores, query_blk = scores_of(start)
        top = jnp.max(scores, axis=-1, keepdims=True)
        expd = jnp.exp(scores - top)
        total = jnp.sum(expd, axis=-1, keepdims=True)
        probs_low = (expd / total).astype(jnp.bfloat16)
        mixed = jnp.einsum(
            "hqk,khc->qhc", probs_low, win_values, preferred_element_type=jnp.float32
        )
        return (
            mixed.astype(jnp.bfloat16).reshape(block, local_width),
            (top + jnp.log(total))[..., 0],
        )

    attended, logsum = lax.map(forward_block, block_starts)
    attended = attended.reshape(rows, local_width)
    attn_part = jnp.einsum("tf,df->td", attended, out_weight, preferred_element_type=jnp.float32)

    def trim(value):
        return mine(value)

    branch = lax.psum(attn_part.astype(jnp.bfloat16), "tensor").astype(
        jnp.float32
    ) + out_bias.astype(jnp.float32)
    middle = tokens_full + gate_a * branch
    normed_m, norm_back_m = jax.vjp(layer_norm, middle)
    entry_m = (normed_m * (1.0 + scale_m) + shift_m).astype(jnp.bfloat16)
    hidden_pre = jnp.dot(entry_m, up_weight, preferred_element_type=jnp.float32) + up_bias.astype(
        jnp.float32
    )
    hidden_full, gelu_back = jax.vjp(gelu_tanh, hidden_pre)
    hidden = hidden_full.astype(jnp.bfloat16)
    mlp_part = jnp.einsum("tf,df->td", hidden, down_weight, preferred_element_type=jnp.float32)
    branch_m = lax.psum(mlp_part.astype(jnp.bfloat16), "tensor").astype(
        jnp.float32
    ) + down_bias.astype(jnp.float32)
    output = trim((middle + gate_m * branch_m).astype(jnp.bfloat16))
    grad_out = out_grad.astype(jnp.float32)
    grad_branch_m = (gate_m * grad_out).astype(jnp.bfloat16)
    grad_gate_m = grad_out * branch_m
    grad_down_b = jnp.sum(grad_branch_m.astype(jnp.float32), axis=0)
    grad_down_w = jnp.einsum("td,tf->df", grad_branch_m, hidden, preferred_element_type=jnp.float32)
    grad_hidden = jnp.einsum(
        "td,df->tf", grad_branch_m, down_weight, preferred_element_type=jnp.float32
    )
    grad_pre = gelu_back(grad_hidden)[0].astype(jnp.bfloat16)
    grad_up_b = jnp.sum(grad_pre.astype(jnp.float32), axis=0)
    grad_up_w = jnp.einsum("td,tf->df", entry_m, grad_pre, preferred_element_type=jnp.float32)
    entry_part = jnp.einsum("tf,df->td", grad_pre, up_weight, preferred_element_type=jnp.float32)
    grad_entry_m = lax.psum(entry_part.astype(jnp.bfloat16), "tensor").astype(jnp.float32)
    grad_middle = grad_out + norm_back_m(grad_entry_m * (1.0 + scale_m))[0]
    grad_gate_a = grad_middle * branch
    grad_branch_part = (gate_a * grad_middle).astype(jnp.bfloat16)
    grad_out_b = jnp.sum(grad_branch_part.astype(jnp.float32), axis=0)
    grad_out_w = jnp.einsum(
        "td,tf->df", grad_branch_part, attended, preferred_element_type=jnp.float32
    )
    grad_attended = jnp.einsum(
        "td,df->tf", grad_branch_part, out_weight, preferred_element_type=jnp.float32
    ).astype(jnp.bfloat16)

    def backward_block(carry, inputs):
        start, logsum_blk = inputs
        scores, query_blk = scores_of(start)
        probs = jnp.exp(scores - logsum_blk[..., None])
        probs_low = probs.astype(jnp.bfloat16)
        grad_blk = lax.dynamic_slice_in_dim(grad_attended, start, block, 0).reshape(
            block, heads_here, HD
        )
        grad_win_values = carry[1] + jnp.einsum(
            "hqk,qhc->khc", probs_low, grad_blk, preferred_element_type=jnp.float32
        )
        grad_probs = jnp.einsum(
            "qhc,khc->hqk", grad_blk, win_values, preferred_element_type=jnp.float32
        )
        grad_scores = (
            probs * (grad_probs - jnp.sum(probs * grad_probs, axis=-1, keepdims=True))
        ).astype(jnp.bfloat16)
        grad_query_blk = (
            jnp.einsum("hqk,khc->qhc", grad_scores, win_keys, preferred_element_type=jnp.float32)
            * factor
        )
        grad_win_keys = (
            carry[0]
            + jnp.einsum("hqk,qhc->khc", grad_scores, query_blk, preferred_element_type=jnp.float32)
            * factor
        )
        return ((grad_win_keys, grad_win_values), grad_query_blk.reshape(block, local_width))

    empty = jnp.zeros((window, heads_here, HD), jnp.float32)
    (grad_win_keys, grad_win_values), grad_query = lax.scan(
        backward_block, (empty, empty), (block_starts, logsum)
    )
    grad_query = grad_query.reshape(rows, local_width)
    grad_pair = jnp.stack([grad_win_keys, grad_win_values]).reshape(
        2, 2 * REACH + 1, rows, local_width
    )
    grad_kv = grad_pair[:, REACH]
    for place, hop in enumerate(hops):
        if hop != 0:
            grad_kv = grad_kv + from_behind(
                grad_pair[:, place].astype(jnp.bfloat16), "dp", -hop
            ).astype(jnp.float32)
    grad_proj = jnp.stack(
        [
            grad_query.astype(jnp.bfloat16),
            grad_kv[0].astype(jnp.bfloat16),
            grad_kv[1].astype(jnp.bfloat16),
        ]
    )
    grad_in_w = jnp.einsum("td,ctf->dcf", entry, grad_proj, preferred_element_type=jnp.float32)
    grad_proj_full = grad_proj.astype(jnp.float32)
    grad_in_b = jnp.stack([jnp.sum(grad_proj_full[0], axis=0), jnp.sum(grad_proj_full[2], axis=0)])
    grad_entry = jnp.einsum("ctf,dcf->td", grad_proj, in_weight, preferred_element_type=jnp.float32)
    input_part = norm_back(grad_entry * (1.0 + scale_a))[0]
    split_terms = jnp.concatenate([grad_entry, grad_entry * normed], axis=1)
    kept_terms = trim(
        jnp.concatenate([grad_gate_a, grad_entry_m, grad_entry_m * normed_m, grad_gate_m], axis=1)
    )
    per_latent = jnp.concatenate(
        [onehot_sum(select, split_terms), onehot_sum(mine(select), kept_terms)], axis=1
    )
    own_count = latents // data_size
    columns_here = mod_weight.shape[1]
    arranged = per_latent.reshape(data_size, own_count, tensor_size, columns_here)
    arranged = arranged.transpose(0, 2, 1, 3).reshape(
        data_size * tensor_size * own_count, columns_here
    )
    grad_mod = lax.psum_scatter(arranged, ("dp", "tensor"), scatter_dimension=0, tiled=True).astype(
        jnp.bfloat16
    )
    own_silu = lax.dynamic_slice_in_dim(silu_cond, data_index * own_count, own_count, 0)
    own_cond = lax.dynamic_slice_in_dim(cond_full, data_index * own_count, own_count, 0)
    grad_mod_w = jnp.einsum("ld,lm->dm", own_silu, grad_mod, preferred_element_type=jnp.float32)
    grad_mod_b = jnp.sum(grad_mod.astype(jnp.float32), axis=0)
    silu_grad = jnp.einsum("lm,dm->ld", grad_mod, mod_weight, preferred_element_type=jnp.float32)
    silu_back = jax.vjp(jax.nn.silu, own_cond)[1]
    cond_part = silu_back(silu_grad)[0]
    placed = lax.dynamic_update_slice_in_dim(
        jnp.zeros((rows, width), jnp.float32), trim(grad_middle), row_start, 0
    )
    grad_tokens, grad_cond = (
        lax.psum_scatter(
            (input_part + placed).astype(jnp.bfloat16), "tensor", scatter_dimension=1, tiled=True
        ).astype(jnp.float32),
        lax.psum_scatter(
            cond_part.astype(jnp.bfloat16), "tensor", scatter_dimension=1, tiled=True
        ).astype(jnp.float32),
    )
    sum_in_b, sum_out_b, sum_up_b, sum_down_b, sum_mod_b = lax.psum(
        (grad_in_b, grad_out_b, grad_up_b, grad_down_b, grad_mod_b), "dp"
    )
    sent_in, sent_out, sent_up, sent_down, sent_mod = (
        lax.psum_scatter(grad_in_w, "dp", scatter_dimension=0, tiled=True),
        lax.psum_scatter(grad_out_w, "dp", scatter_dimension=0, tiled=True),
        lax.psum_scatter(grad_up_w, "dp", scatter_dimension=0, tiled=True),
        lax.psum_scatter(grad_down_w, "dp", scatter_dimension=0, tiled=True),
        lax.psum_scatter(grad_mod_w, "dp", scatter_dimension=0, tiled=True),
    )
    return (
        output,
        grad_tokens,
        grad_cond,
        sent_in,
        sum_in_b,
        sent_out,
        sum_out_b,
        sent_up,
        sum_up_b,
        sent_down,
        sum_down_b,
        sent_mod,
        sum_mod_b,
    )


def solution(mesh):
    placed = (
        P("dp", None),
        P(),
        P(),
        P(None, None, "tensor"),
        P(None, "tensor"),
        P(None, "tensor"),
        P(),
        P(None, "tensor"),
        P("tensor"),
        P(None, "tensor"),
        P(),
        P(None, "tensor"),
        P("tensor"),
        P("dp", None),
    )
    return jax.shard_map(
        on_device,
        mesh=mesh,
        in_specs=placed,
        out_specs=(
            P(("dp", "tensor"), None),
            P("dp", "tensor"),
            P("dp", "tensor"),
            P("dp", None, "tensor"),
            P(None, "tensor"),
            P("dp", "tensor"),
            P(),
            P("dp", "tensor"),
            P("tensor"),
            P("dp", "tensor"),
            P(),
            P("dp", "tensor"),
            P("tensor"),
        ),
        check_vma=False,
    )
```

profile of v0, /device:TPU:0, one launch (start us, length us, event | category | flops | bytes accessed | tf_op | source)
XLA Modules:
  0.0 1369.8 jit_solution(1192815745939102613)
XLA Ops:
  16.4 7.0 all-gather
  23.7 11.5 fusion.64
  35.3 20.4 %fusion.91 = (f32[1024,1,1152]{0,2,1:T(8,128)}, f32[1024,1,1152]{0,2,1:T(8,128)}, f32[1024,1,1152]{0,2,1:T(8,128)}, f32[1024,1,1152]{0,2,1:T(8,128)}, f32[1024,1,1152]{0,2,1:T(8,128)}, /*index=5*/f32[1024,1,1152]{0,2,1:T(8,128)}) fusion(f32[1024,6,1152]{0,2,1:T(8,128)} %bitcast.203), kind=kLoop, calls=%fused_computation.182 | loop fusion | bytes 56623104 | tf_op jit(solution)/shard_map/slice | solution.py:92
  86.8 21.8 %collective-permute-done.1 = bf16[2,1024,288]{1,2,0:T(8,128)(2,1)} collective-permute-done((bf16[2,1024,288]{1,2,0:T(8,128)(2,1)}, bf16[2,1024,288]{1,2,0:T(8,128)(2,1)}, u32[]{:S(2)}, u32[]{:S(2)}) %collective-permute-start.1) | collective-permute-done | bytes 1179680 | tf_op jit(solution)/shard_map/ppermute | solution.py:13
  108.5 25.3 %collective-permute-done = bf16[2,1024,288]{1,2,0:T(8,128)(2,1)} collective-permute-done((bf16[2,1024,288]{1,2,0:T(8,128)(2,1)}, bf16[2,1024,288]{1,2,0:T(8,128)(2,1)}, u32[]{:S(2)}, u32[]{:S(2)}) %collective-permute-start) | collective-permute-done | bytes 1179680 | tf_op jit(solution)/shard_map/ppermute | solution.py:13
  138.0 82.1 %while.27 = (s32[]{:T(128)}, bf16[2,512,288]{1,2,0:T(8,128)(2,1)}, f32[2,4,512]{2,1,0:T(4,128)S(1)}, s32[2]{0:T(128)S(1)}, s32[1024]{0:T(1024)S(1)}, /*index=5*/...) while((s32[]{:T(128)}, bf16[2,512,288]{1,2,0:T(8,128)(2,1)}, ...), condition=%wide.region_8.9_spmd, body=%wide.region_5.8_spmd.sunk | while | flops 1889155072 | bytes 98978056 | solution.py:139
  141.7 12.7 fusion.156
  154.4 12.0 fusion.157
  166.4 11.8 fusion.158
  182.8 12.7 fusion.156
  195.5 12.0 fusion.157
  207.5 11.8 fusion.158
  233.0 6.2 copy.96
  245.3 6.1 copy.97
  262.5 20.9 %all-reduce.7.cloned.1.call-done = bf16[1024,1152]{1,0:T(8,128)(2,1)} async-done(((bf16[1024,1152]{1,0:T(8,128)(2,1)}), bf16[1024,1152]{1,0:T(8,128)(2,1)}) %all-reduce.7.cloned.1.call-update) | async-done | bytes 2359312 | tf_op jit(solution)/shard_map/psum | solution.py:146
  288.8 6.4 fusion.44
  295.3 6.3 convert_reduce_fusion.2
  314.4 92.2 %all-reduce.9.cloned.1.call-done = (bf16[1024,1152]{1,0:T(8,128)(2,1)}, bf16[1024,1152]{1,0:T(8,128)(2,1)}) async-done(((bf16[1024,1152]{1,0:T(8,128)(2,1)}, bf16[1024,1152]{1,0:T(8,128)(2,1)}), (bf16[1024,1152]{1,0:T(8,128)(2,1)}, bf16[1024,1152]{1,0:T(8,128)(2,1)})) %all-reduce.9.cloned.1.call-update) | async-done | bytes 4718608 | tf_op jit(solution)/shard_map/psum | solution.py:174
  420.6 6.5 convert_multiply_fusion
  429.5 182.3 %while.28 = (s32[]{:T(128)}, f32[3072,4,72]{0,2,1:T(8,128)}, f32[3072,4,72]{0,2,1:T(8,128)}, bf16[2,512,288]{1,2,0:T(8,128)(2,1)}, s32[2]{0:T(128)S(1)}, /*index...) while((s32[]{:T(128)}, f32[3072,4,72]{0,2,1:T(8,128)}, ...), condition=%wide.region_18.19_spmd.clone, body=%wide.region_16.18_spmd.clone.sunk | while | flops 4630509568 | bytes 227256688 | solution.py:215
  433.9 11.6 fusion.169
  445.5 13.7 %fusion.171 = f32[3072,4,72]{0,2,1:T(8,128)} fusion(bf16[512,4,72]{0,2,1:T(8,128)(2,1)S(1)} %bitcast.207, f32[4,512,3072]{2,1,0:T(8,128)} %fusion.169, f32[4,512]{1,0:T(4,128)S(1)} %dynamic-slice_bitcast_fusion.2, pred[512,3072]{1,0:T(8,128)(4,1)S(1)} %broadcast_compare_fusion.5, f32[3072,4,72]{0,2,1:T(8,128)} %get-tuple-element.508, pred[]{:T(512)S(6)} %compare.3), kind=kOutput, calls=%fused_computation.23.clone.1 | convolution fusion | flops 932904960 | bytes 34119680 | tf_op jit(solution)/shard_map/while/body/eval_jaxpr/hqk,qhc->khc/dot_general | solution.py:194
  459.3 20.4 %multiply_reduce_fusion.4 = (f32[4,512]{1,0:T(4,128)S(1)}, f32[4,512,3072]{2,1,0:T(8,128)}) fusion(f32[4,512,3072]{2,1,0:T(8,128)} %fusion.169, f32[4,512]{1,0:T(4,128)S(1)} %dynamic-slice_bitcast_fusion.2, pred[512,3072]{1,0:T(8,128)(4,1)S(1)} %broadcast_compare_fusion.5, bf16[512,4,72]{0,2,1:T(8,128)(2,1)S(1)} %bitcast.208, ...), kind=kOutput, calls=%fused_computation.14.clone.1 | convolution fusion | flops 937424896 | bytes 53985280 | tf_op jit(solution)/shard_map/while/body/eval_jaxpr/qhc,khc->hqk/dot_general | solution.py:197
  479.7 21.3 %multiply_convert_fusion.7 = bf16[4,512,3072]{2,1,0:T(8,128)(2,1)} fusion(f32[4,512,3072]{2,1,0:T(8,128)} %get-tuple-element.453, f32[4,512,3072]{2,1,0:T(8,128)} %fusion.169, f32[4,512]{1,0:T(4,128)S(1)} %get-tuple-element.454, f32[4,512]{1,0:T(4,128)S(1)} %dynamic-slice_bitcast_fusion.2, pred[512,3072]{1,0:T(8,128)(4,1)S(1)} %broadcast_compare_fusion.5), kind=kLoop, calls=%fused_computation.13.clone.1 | loop fusion | flops 37748736 | bytes 64503808 | tf_op jit(solution)/shard_map/while/body/eval_jaxpr/convert_element_type | solution.py:202
  501.0 9.0 convolution_multiply_fusion.3
  510.0 8.9 fusion.170
  523.7 11.6 fusion.169
  535.4 14.7 %fusion.171 = f32[3072,4,72]{0,2,1:T(8,128)} fusion(bf16[512,4,72]{0,2,1:T(8,128)(2,1)S(1)} %bitcast.207, f32[4,512,3072]{2,1,0:T(8,128)} %fusion.169, f32[4,512]{1,0:T(4,128)S(1)} %dynamic-slice_bitcast_fusion.2, pred[512,3072]{1,0:T(8,128)(4,1)S(1)} %broadcast_compare_fusion.5, f32[3072,4,72]{0,2,1:T(8,128)} %get-tuple-element.508, pred[]{:T(512)S(6)} %compare.3), kind=kOutput, calls=%fused_computation.23.clone.1 | convolution fusion | flops 932904960 | bytes 34119680 | tf_op jit(solution)/shard_map/while/body/eval_jaxpr/hqk,qhc->khc/dot_general | solution.py:194
  550.1 20.4 %multiply_reduce_fusion.4 = (f32[4,512]{1,0:T(4,128)S(1)}, f32[4,512,3072]{2,1,0:T(8,128)}) fusion(f32[4,512,3072]{2,1,0:T(8,128)} %fusion.169, f32[4,512]{1,0:T(4,128)S(1)} %dynamic-slice_bitcast_fusion.2, pred[512,3072]{1,0:T(8,128)(4,1)S(1)} %broadcast_compare_fusion.5, bf16[512,4,72]{0,2,1:T(8,128)(2,1)S(1)} %bitcast.208, ...), kind=kOutput, calls=%fused_computation.14.clone.1 | convolution fusion | flops 937424896 | bytes 53985280 | tf_op jit(solution)/shard_map/while/body/eval_jaxpr/qhc,khc->hqk/dot_general | solution.py:197
  570.5 21.3 %multiply_convert_fusion.7 = bf16[4,512,3072]{2,1,0:T(8,128)(2,1)} fusion(f32[4,512,3072]{2,1,0:T(8,128)} %get-tuple-element.453, f32[4,512,3072]{2,1,0:T(8,128)} %fusion.169, f32[4,512]{1,0:T(4,128)S(1)} %get-tuple-element.454, f32[4,512]{1,0:T(4,128)S(1)} %dynamic-slice_bitcast_fusion.2, pred[512,3072]{1,0:T(8,128)(4,1)S(1)} %broadcast_compare_fusion.5), kind=kLoop, calls=%fused_computation.13.clone.1 | loop fusion | flops 37748736 | bytes 64503808 | tf_op jit(solution)/shard_map/while/body/eval_jaxpr/convert_element_type | solution.py:202
  591.8 9.0 convolution_multiply_fusion.3
  600.9 9.9 fusion.170
  613.9 6.6 stack.30
  620.5 6.2 copy_dynamic-update-slice_fusion.1
  626.7 6.6 stack.31
  633.3 6.3 copy_dynamic-update-slice_fusion
  656.3 18.6 %collective-permute-done.2 = bf16[2,1024,288]{1,2,0:T(8,128)(2,1)S(1)} collective-permute-done((bf16[2,1024,288]{1,2,0:T(8,128)(2,1)}, bf16[2,1024,288]{1,2,0:T(8,128)(2,1)S(1)}, u32[]{:S(2)}, u32[]{:S(2)}) %collective-permute-start.2) | collective-permute-done | bytes 1179680 | tf_op jit(solution)/shard_map/ppermute | solution.py:13
  674.9 25.3 %collective-permute-done.3 = bf16[2,1024,288]{1,2,0:T(8,128)(2,1)} collective-permute-done((bf16[2,1024,288]{1,2,0:T(8,128)(2,1)}, bf16[2,1024,288]{1,2,0:T(8,128)(2,1)}, u32[]{:S(2)}, u32[]{:S(2)}) %collective-permute-start.3) | collective-permute-done | bytes 1179680 | tf_op jit(solution)/shard_map/ppermute | solution.py:13
  713.5 46.7 %all-reduce.10 = bf16[64,1728]{1,0:T(8,128)(2,1)S(1)} all-reduce(f32[64,1728]{1,0:T(8,128)S(1)} %reshape.261), channel_id=3, replica_groups=mesh['dp'=8,'tensor'=4] {'dp','tensor'}, use_global_device_ids=true, to_apply=%region_22.23.clone | all-reduce | flops 110592 | bytes 663552
  776.1 7.3 fusion.96
  785.1 8.0 fusion.84
  794.4 7.3 fusion.63
  811.0 36.7 %all-reduce.1 = (f32[2,288]{1,0:T(2,128)}, f32[1152]{0:T(1024)}, f32[1152]{0:T(1024)}, f32[1152]{0:T(1024)}, f32[1728]{0:T(1024)}) all-reduce(f32[2,288]{1,0:T(2,128)S(1)} %pad_maximum_fusion.7, f32[1152]{0:T(1024)S(1)} %copy-done.42, f32[1152]{0:T(1024)S(1)} %copy-done.44, ...), channel_id=1, replica_groups=mesh['dp'=8,'tensor'=4] {'dp'}, use_global_device_ids=true, to_apply=%region_27.28 | all-reduce | flops 5760 | bytes 46080 | tf_op jit(solution)/shard_map/psum | solution.py:274
  852.0 36.1 %reduce-scatter.14.cloned.1.call-done = f32[144,288]{1,0:T(8,128)} async-done(((f32[1152,288]{1,0:T(8,128)}), f32[144,288]{1,0:T(8,128)}) %reduce-scatter.14.cloned.1.call-update) | async-done | bytes 165904 | tf_op jit(solution)/shard_map/reduce_scatter | solution.py:279
  888.1 107.3 %reduce-scatter.16.cloned.1.call-done = f32[144,1152]{1,0:T(8,128)} async-done(((f32[1152,1152]{1,0:T(8,128)}), f32[144,1152]{1,0:T(8,128)}) %reduce-scatter.16.cloned.1.call-update) | async-done | bytes 663568 | tf_op jit(solution)/shard_map/reduce_scatter | solution.py:280
  995.4 108.1 %reduce-scatter.18.cloned.1.call-done = f32[144,1152]{1,0:T(8,128)} async-done(((f32[1152,1152]{1,0:T(8,128)}), f32[144,1152]{1,0:T(8,128)}) %reduce-scatter.18.cloned.1.call-update) | async-done | bytes 663568 | tf_op jit(solution)/shard_map/reduce_scatter | solution.py:281
  1103.5 108.4 %reduce-scatter.12.cloned.1.call-done = f32[144,3,288]{2,0,1:T(8,128)} async-done(((f32[1152,3,288]{2,0,1:T(8,128)}), f32[144,3,288]{2,0,1:T(8,128)}) %reduce-scatter.12.cloned.1.call-update) | async-done | bytes 497680 | tf_op jit(solution)/shard_map/reduce_scatter | solution.py:278
  1211.9 150.9 %reduce-scatter.20.cloned.1.call-done = f32[144,1728]{1,0:T(8,128)} async-done(((f32[1152,1728]{1,0:T(8,128)}), f32[144,1728]{1,0:T(8,128)}) %reduce-scatter.20.cloned.1.call-update) | async-done | bytes 995344 | tf_op jit(solution)/shard_map/reduce_scatter | solution.py:282
  (309 shorter events, 183.8 us)
Async XLA Ops:
  7.2 288.0 %copy-start = (bf16[1152,1152]{1,0:T(8,128)(2,1)S(1)}, bf16[1152,1152]{1,0:T(8,128)(2,1)}, u32[]{:S(2)}) copy-start(bf16[1152,1152]{1,0:T(8,128)(2,1)} %param.25) | copy-start | bytes 7962628
  7.2 276.2 %all-reduce.7.cloned.1.call-start = ((), (), s32[]{:S(2)}) async-start(), calls=%async_computation.7 | async-start | bytes 4718592 | tf_op jit(solution)/shard_map/psum | solution.py:146
  10.2 57.7 %copy-start.36 = (f32[1024]{0:T(1024)}, f32[1024]{0:T(1024)S(1)}, u32[]{:S(2)}) copy-start(f32[1024]{0:T(1024)S(1)} %broadcast_multiply_fusion.1) | copy-start | bytes 12292
  12.7 55.2 %copy-start.38 = (f32[1024]{0:T(1024)}, f32[1024]{0:T(1024)S(1)}, u32[]{:S(2)}) copy-start(f32[1024]{0:T(1024)S(1)} %fusion.75) | copy-start | bytes 12292
  78.1 30.4 %collective-permute-start.1 = (bf16[2,1024,288]{1,2,0:T(8,128)(2,1)}, bf16[2,1024,288]{1,2,0:T(8,128)(2,1)}, u32[]{:S(2)}, u32[]{:S(2)}) collective-permute-start(bf16[2,1024,288]{1,2,0:T(8,128)(2,1)} %pad_maximum_fusion.3), channel_id=1, source_target_pairs={{4,0},{8,4},{12,8},{16,12},{20,16},{24,20},{28,24},{5,1},{9,5},{13... | collective-permute-start | bytes 3538952 | tf_op jit(solution)/shard_map/ppermute | solution.py:13
  79.4 54.5 %collective-permute-start = (bf16[2,1024,288]{1,2,0:T(8,128)(2,1)}, bf16[2,1024,288]{1,2,0:T(8,128)(2,1)}, u32[]{:S(2)}, u32[]{:S(2)}) collective-permute-start(bf16[2,1024,288]{1,2,0:T(8,128)(2,1)} %pad_maximum_fusion.3), channel_id=1, source_target_pairs={{0,4},{4,8},{8,12},{12,16},{16,20},{20,24},{24,28},{1,5},{5,9},{9,... | collective-permute-start | bytes 3538952 | tf_op jit(solution)/shard_map/ppermute | solution.py:13
  154.4 12.0 copy-start.3
  166.4 11.8 copy-start.28
  195.5 12.0 copy-start.3
  207.5 11.8 copy-start.28
  220.2 12.8 copy-start.6
  220.2 6.7 copy-start.46
  220.2 6.7 copy-start.47
  226.4 180.2 %all-reduce.9.cloned.1.call-start = ((), (), s32[]{:S(2)}) async-start(), calls=%async_computation.15 | async-start | bytes 9437184 | tf_op jit(solution)/shard_map/psum | solution.py:174
  226.9 56.5 %copy-start.34 = (f32[1152]{0:T(1024)}, f32[1152]{0:T(1024)S(1)}, u32[]{:S(2)}) copy-start(f32[1152]{0:T(1024)S(1)} %convert_element_type.195) | copy-start | bytes 13828
  288.2 7.1 copy-start.2
  288.2 7.1 slice-start.12
  288.8 6.5 slice-start.13
  295.3 6.3 copy-start.18
  312.1 102.8 %slice-start = ((s8[4718592]{0:T(1024)(128)(4,1)}), s8[524288]{0:T(1024)(128)(4,1)S(1)}, s32[]{:S(2)}) async-start(s8[4718592]{0:T(1024)(128)(4,1)} %bitcast.200), calls=%async_computation.16 | async-start | bytes 1048576
  312.1 535.6 %reduce-scatter.24.cloned.1.call-start = ((), (), s32[]{:S(2)}) async-start(), calls=%async_computation.14 | async-start | bytes 368640
  406.6 8.3 slice-start.1
  412.2 8.3 slice-start.2
  420.6 8.0 copy-start.54
  510.0 8.9 copy-start.26
  510.0 9.8 copy-start.16
  600.8 9.9 copy-start.26
  600.8 10.8 copy-start.16
  633.3 18.9 %slice-start.6 = ((s8[4718592]{0:T(1024)(128)(4,1)}), s8[4194304]{0:T(1024)(128)(4,1)S(1)}, s32[]{:S(2)}) async-start(s8[4718592]{0:T(1024)(128)(4,1)} %bitcast.213), calls=%async_computation.22 | async-start | bytes 8388608
  639.6 12.6 slice-start.7
  639.6 12.6 copy-start.9
  639.6 12.6 copy-start.35
  643.4 9.4 slice-start.8
  643.4 9.4 slice-start.10
  645.0 29.9 %collective-permute-start.2 = (bf16[2,1024,288]{1,2,0:T(8,128)(2,1)}, bf16[2,1024,288]{1,2,0:T(8,128)(2,1)S(1)}, u32[]{:S(2)}, u32[]{:S(2)}) collective-permute-start(bf16[2,1024,288]{1,2,0:T(8,128)(2,1)} %get-tuple-element.303), channel_id=1, source_target_pairs={{4,0},{8,4},{12,8},{16,12},{20,16},{24,20},{28,24},{5,1},{9,5},{13... | collective-permute-start | bytes 3538952 | tf_op jit(solution)/shard_map/ppermute | solution.py:13
  646.6 53.6 %collective-permute-start.3 = (bf16[2,1024,288]{1,2,0:T(8,128)(2,1)}, bf16[2,1024,288]{1,2,0:T(8,128)(2,1)}, u32[]{:S(2)}, u32[]{:S(2)}) collective-permute-start(bf16[2,1024,288]{1,2,0:T(8,128)(2,1)} %get-tuple-element.304), channel_id=1, source_target_pairs={{0,4},{4,8},{8,12},{12,16},{16,20},{20,24},{24,28},{1,5},{5,9},{9,... | collective-permute-start | bytes 3538952 | tf_op jit(solution)/shard_map/ppermute | solution.py:13
  655.3 47.5 %slice-start.4 = ((s8[4718592]{0:T(1024)(128)(4,1)}), s8[4194304]{0:T(1024)(128)(4,1)S(1)}, s32[]{:S(2)}) async-start(s8[4718592]{0:T(1024)(128)(4,1)} %bitcast.211), calls=%async_computation.20 | async-start | bytes 8388608
  655.8 47.0 %copy-start.4 = (bf16[1024,1152]{1,0:T(8,128)(2,1)S(1)}, bf16[1024,1152]{1,0:T(8,128)(2,1)}, u32[]{:S(2)}) copy-start(bf16[1024,1152]{1,0:T(8,128)(2,1)} %param.18) | copy-start | bytes 7077892
  655.8 47.0 %slice-start.5 = ((s8[4718592]{0:T(1024)(128)(4,1)}), s8[524288]{0:T(1024)(128)(4,1)S(1)}, s32[]{:S(2)}) async-start(s8[4718592]{0:T(1024)(128)(4,1)} %bitcast.211), calls=%async_computation.21 | async-start | bytes 1048576
  655.8 47.0 %copy-start.37 = (f32[1024]{0:T(1024)S(1)}, f32[1024]{0:T(1024)}, u32[]{:S(2)}) copy-start(f32[1024]{0:T(1024)} %copy-done.36) | copy-start | bytes 12292
  655.8 47.0 %copy-start.53 = (bf16[1152,3,288]{0,2,1:T(8,128)(2,1)S(1)}, bf16[1152,3,288]{0,2,1:T(8,128)(2,1)}, u32[]{:S(2)}) copy-start(bf16[1152,3,288]{0,2,1:T(8,128)(2,1)} %param.21) | copy-start | bytes 5971972
  764.0 85.3 %reduce-scatter.22.cloned.1.call-start = ((), (), s32[]{:S(2)}) async-start(), calls=%async_computation.13 | async-start | bytes 2949120
  771.3 116.8 %reduce-scatter.14.cloned.1.call-start = ((), (), s32[]{:S(2)}) async-start(), calls=%async_computation.9 | async-start | bytes 1990656 | tf_op jit(solution)/shard_map/reduce_scatter | solution.py:279
  776.0 219.4 %reduce-scatter.16.cloned.1.call-start = ((), (), s32[]{:S(2)}) async-start(), calls=%async_computation.10 | async-start | bytes 5971968 | tf_op jit(solution)/shard_map/reduce_scatter | solution.py:280
  783.4 320.1 %reduce-scatter.18.cloned.1.call-start = ((), (), s32[]{:S(2)}) async-start(), calls=%async_computation.11 | async-start | bytes 5971968 | tf_op jit(solution)/shard_map/reduce_scatter | solution.py:281
  793.1 418.8 %reduce-scatter.12.cloned.1.call-start = ((), (), s32[]{:S(2)}) async-start(), calls=%async_computation.8 | async-start | bytes 5971968 | tf_op jit(solution)/shard_map/reduce_scatter | solution.py:278
  801.8 561.0 %reduce-scatter.20.cloned.1.call-start = ((), (), s32[]{:S(2)}) async-start(), calls=%async_computation.12 | async-start | bytes 9289728 | tf_op jit(solution)/shard_map/reduce_scatter | solution.py:282
  807.1 555.7 %copy-start.1 = (bf16[1152,1152]{1,0:T(8,128)(2,1)S(1)}, bf16[1152,1152]{1,0:T(8,128)(2,1)}, u32[]{:S(2)}) copy-start(bf16[1152,1152]{1,0:T(8,128)(2,1)} %param.25) | copy-start | bytes 7962628
  (43 other events, 125.4 us)
Sparse Core Ops, SparseCore 0:
  226.5 56.8 all-reduce.6
  312.2 94.2 all-reduce.8
  764.1 18.5 reduce-scatter.23
  785.2 33.0 reduce-scatter.21
  822.2 65.8 reduce-scatter.13
  892.5 102.8 reduce-scatter.15
  999.6 103.8 reduce-scatter.17
  1108.1 103.7 reduce-scatter.11
  1216.2 146.5 reduce-scatter.19
where the time goes:
time: 1380 us; the launch traced here: 1370 us
  waiting for transfers between devices  715 us (52%)
  matrix products  263 us (19%)
  other arithmetic  146 us (11%)
  local copies, waits for them, and re-layouts  115 us (8%)
  blocking collectives  90.4 us (7%)
  starting transfers between devices  15.4 us (1%)
  between operations  15.3 us (1%)
    reduce_scatter x1, waiting for transfers between devices, on_device(): lax.psum_scatter(grad_mod_w, 'dp', scatter_dimension=0, tiled=True)  151 us
    reduce_scatter x1, waiting for transfers between devices, on_device(): lax.psum_scatter(grad_in_w, 'dp', scatter_dimension=0, tiled=True)  108 us
    reduce_scatter x1, waiting for transfers between devices, on_device(): lax.psum_scatter(grad_down_w, 'dp', scatter_dimension=0, tiled=True)  108 us
    reduce_scatter x1, waiting for transfers between devices, on_device(): lax.psum_scatter(grad_up_w, 'dp', scatter_dimension=0, tiled=True)  107 us
    psum x1, waiting for transfers between devices, on_device(): lax.psum(entry_part.astype(jnp.bfloat16), 'tensor').astype(jnp.float32)  92.2 us
    ppermute x4, waiting for transfers between devices, from_behind(): return lax.ppermute(block, axis, route)  91 us
    unnamed x141, local copies, waits for them, and re-layouts  59.8 us
    dot_general x4, matrix products, scores_of(): jnp.einsum('qhc,khc->hqk', query_blk, win_keys, preferred_element_type=jn...  48.6 us
  transfers between devices with their start and end apart: 13, of which 11 were waited for; matrix products, arithmetic and copies ran while one was open for 6% of the time, Pallas kernels for 0%

commit v1 on v0

v1 whole, which is shorter than its diff:
```python
import functools
import math

import jax
import jax.numpy as jnp
from jax import lax
from jax.experimental import pallas as pl
from jax.experimental.pallas import tpu as pltpu
from jax.sharding import PartitionSpec as P

HD = 72
FACTOR = HD ** (-0.5)
LOG2E = math.log2(math.e)
NEG = -1e30
BQ = 256
BK = 256
F32 = jnp.float32
BF16 = jnp.bfloat16


def contract(a, b, dims):
    return lax.dot_general(a, b, (dims, ((), ())), preferred_element_type=F32)


def forward_kernel(bases, heads, bounds, span, query, *refs):
    segments = len(bases)
    keys = refs[:segments]
    values = refs[segments : 2 * segments]
    out, logsum, mixed = refs[2 * segments :]
    rows = query.shape[2]
    scale = FACTOR * LOG2E

    def query_block(i, _):
        at = pl.multiple_of(i * BQ, BQ)
        own = pl.ds(at, BQ)
        begin = span[0:1, own]
        end = span[1:2, own]
        q = [query[h, :, own] for h in range(heads)]
        mixed[...] = jnp.zeros_like(mixed)
        state = tuple(jnp.full((1, BQ), NEG, F32) for _ in range(heads)) + tuple(
            jnp.zeros((1, BQ), F32) for _ in range(heads)
        )
        for s, base in enumerate(bases):

            def key_block(j, state, s=s, base=base):
                k_at = pl.multiple_of(j * BK, BK)
                block = pl.ds(k_at, BK)
                place = lax.broadcasted_iota(jnp.int32, (BK, BQ), 0) + (k_at + base)
                allowed = (place >= begin) & (place < end)
                tops, totals = [], []
                for h in range(heads):
                    raw = contract(keys[s][h, :, block], q[h], ((0,), (0,)))
                    raw = jnp.where(allowed, raw * scale, NEG)
                    top = jnp.maximum(state[h], jnp.max(raw, axis=0, keepdims=True))
                    probs = jnp.exp2(raw - top)
                    shrink = jnp.exp2(state[h] - top)
                    tops.append(top)
                    totals.append(state[heads + h] * shrink + jnp.sum(probs, axis=0, keepdims=True))
                    mixed[h] = mixed[h] * shrink + contract(
                        values[s][h, :, block], probs.astype(BF16), ((1,), (0,))
                    )
                return tuple(tops) + tuple(totals)

            state = lax.fori_loop(bounds[s, 0, i], bounds[s, 1, i], key_block, state)
        for h in range(heads):
            total = state[heads + h]
            out[h, :, own] = (mixed[h] / total).astype(BF16)
            logsum[h, :, own] = state[h] + jnp.log2(total)
        return 0

    lax.fori_loop(0, rows // BQ, query_block, 0)


def attend(bounds, span, query, keys, values, bases):
    heads, hd, rows = query.shape
    vmem = pl.BlockSpec(memory_space=pltpu.VMEM)
    return pl.pallas_call(
        functools.partial(forward_kernel, bases, heads),
        out_shape=(
            jax.ShapeDtypeStruct((heads, hd, rows), BF16),
            jax.ShapeDtypeStruct((heads, 1, rows), F32),
        ),
        in_specs=[pl.BlockSpec(memory_space=pltpu.SMEM)] + [vmem] * (2 + 2 * len(bases)),
        out_specs=(vmem, vmem),
        scratch_shapes=[pltpu.VMEM((heads, hd, BQ), F32)],
        compiler_params=pltpu.CompilerParams(vmem_limit_bytes=40 << 20),
        cost_estimate=pl.CostEstimate(
            flops=24 * heads * rows * rows * HD,
            bytes_accessed=12 << 20,
            transcendentals=heads * rows * rows,
        ),
    )(bounds, span, query, *keys, *values)


def backward_kernel(bases, heads, bounds, span, query, grad, attended, logsum, *refs):
    segments = len(bases)
    keys = refs[:segments]
    values = refs[segments : 2 * segments]
    grad_query = refs[2 * segments]
    grad_keys = refs[2 * segments + 1 : 3 * segments + 1]
    grad_values = refs[3 * segments + 1 : 4 * segments + 1]
    delta, sum_query, sum_keys, sum_values = refs[4 * segments + 1 :]
    scale = FACTOR * LOG2E
    rows = query.shape[2]
    for h in range(heads):
        delta[h] = jnp.sum(
            grad[h].astype(F32) * attended[h].astype(F32), axis=0, keepdims=True
        )
    sum_query[...] = jnp.zeros_like(sum_query)
    for s, base in enumerate(bases):

        def key_block(j, _, s=s, base=base):
            k_at = pl.multiple_of(j * BK, BK)
            block = pl.ds(k_at, BK)
            place = lax.broadcasted_iota(jnp.int32, (BK, BQ), 0) + (k_at + base)
            sum_keys[...] = jnp.zeros_like(sum_keys)
            sum_values[...] = jnp.zeros_like(sum_values)

            def query_block(i, _):
                own = pl.ds(pl.multiple_of(i * BQ, BQ), BQ)
                allowed = (place >= span[0:1, own]) & (place < span[1:2, own])
                for h in range(heads):
                    k = keys[s][h, :, block]
                    q = query[h, :, own]
                    g = grad[h, :, own]
                    raw = contract(k, q, ((0,), (0,)))
                    raw = jnp.where(allowed, raw * scale - logsum[h, :, own], NEG)
                    probs = jnp.exp2(raw)
                    grad_probs = contract(values[s][h, :, block], g, ((0,), (0,)))
                    grad_raw = (probs * (grad_probs - delta[h, :, own])).astype(BF16)
                    sum_values[h] += contract(g, probs.astype(BF16), ((1,), (1,)))
                    sum_keys[h] += contract(q, grad_raw, ((1,), (1,)))
                    sum_query[h, :, own] += contract(k, grad_raw, ((1,), (0,)))
                return 0

            lax.fori_loop(bounds[s, 0, j], bounds[s, 1, j], query_block, 0)
            for h in range(heads):
                grad_keys[s][h, :, block] = (sum_keys[h] * FACTOR).astype(BF16)
                grad_values[s][h, :, block] = sum_values[h].astype(BF16)
            return 0

        lax.fori_loop(0, keys[s].shape[2] // BK, key_block, 0)
    grad_query[...] = (sum_query[...] * FACTOR).astype(BF16)


def attend_back(bounds, span, query, grad, attended, logsum, keys, values, bases):
    heads, hd, rows = query.shape
    segments = len(bases)
    vmem = pl.BlockSpec(memory_space=pltpu.VMEM)
    shape = jax.ShapeDtypeStruct((heads, hd, rows), BF16)
    found = pl.pallas_call(
        functools.partial(backward_kernel, bases, heads),
        out_shape=(shape,) * (1 + 2 * segments),
        in_specs=[pl.BlockSpec(memory_space=pltpu.SMEM)] + [vmem] * (5 + 2 * segments),
        out_specs=(vmem,) * (1 + 2 * segments),
        scratch_shapes=[
            pltpu.VMEM((heads, 1, rows), F32),
            pltpu.VMEM((heads, hd, rows), F32),
            pltpu.VMEM((heads, hd, BK), F32),
            pltpu.VMEM((heads, hd, BK), F32),
        ],
        compiler_params=pltpu.CompilerParams(vmem_limit_bytes=44 << 20),
        cost_estimate=pl.CostEstimate(
            flops=60 * heads * rows * rows * HD,
            bytes_accessed=24 << 20,
            transcendentals=heads * rows * rows,
        ),
    )(bounds, span, query, grad, attended, logsum, *keys, *values)
    return found[0], found[1 : 1 + segments], found[1 + segments :]


def swap(value, axis, bit):
    return lax.ppermute(value, axis, [(i, i ^ bit) for i in range(lax.axis_size(axis))])


def shift(value, axis, distance):
    devices = range(lax.axis_size(axis))
    return lax.ppermute(value, axis, [(i, i + distance) for i in devices if i + distance in devices])


def bits_of(axis):
    size = lax.axis_size(axis)
    return [1 << b for b in range(size.bit_length() - 1)]


def bit_set(axis, bit):
    return (lax.axis_index(axis) & bit) != 0


def sum_all(value, axis):
    for bit in bits_of(axis):
        value = value + swap(value, axis, bit)
    return value


def in_order(mine, other, upper, dim=0):
    return jnp.where(
        upper, jnp.stack([other, mine], axis=dim), jnp.stack([mine, other], axis=dim)
    )


def gather_tensor(value):
    pair = in_order(value, swap(value, "tensor", 2), bit_set("tensor", 2))
    quad = in_order(pair, swap(pair, "tensor", 1), bit_set("tensor", 1), dim=1)
    return quad.reshape((4 * value.shape[0],) + value.shape[1:])


def scatter_tensor(partial):
    n = partial.shape[0] // 4
    core = lax.axis_index("tensor") % 2
    across = lax.axis_index("tensor") // 2
    parts = partial.astype(BF16).reshape((2, 2, n) + partial.shape[1:])
    kept = lax.dynamic_index_in_dim(parts, core, 1, keepdims=False)
    sent = lax.dynamic_index_in_dim(parts, 1 - core, 1, keepdims=False)
    half = kept.astype(F32) + swap(sent, "tensor", 1).astype(F32)
    half_low = half.astype(BF16)
    stay = lax.dynamic_index_in_dim(half, across, 0, keepdims=False)
    leave = lax.dynamic_index_in_dim(half_low, 1 - across, 0, keepdims=False)
    return stay + swap(leave, "tensor", 2).astype(F32)


def scatter_data(partial):
    size = lax.axis_size("dp")
    if size != 8:
        return lax.psum_scatter(
            partial.astype(BF16), "dp", scatter_dimension=0, tiled=True
        ).astype(F32)
    index = lax.axis_index("dp")
    near, far = index % 2, index // 2
    rows = partial.shape[0] // 8
    parts = partial.astype(BF16).reshape((4, 2, rows) + partial.shape[1:])
    kept = lax.dynamic_index_in_dim(parts, near, 1, keepdims=False)
    sent = lax.dynamic_index_in_dim(parts, 1 - near, 1, keepdims=False)
    half = kept.astype(F32) + swap(sent, "dp", 1).astype(F32)
    half_low = half.astype(BF16)
    total = lax.dynamic_index_in_dim(half, far, 0, keepdims=False)
    for step in (1, -1, 2, -2, 3, -3):
        part = lax.dynamic_index_in_dim(half_low, jnp.clip(far + step, 0, 3), 0, keepdims=False)
        total = total + shift(part, "dp", 2 * step).astype(F32)
    return total


def layer_norm(value):
    center = value - jnp.mean(value, axis=-1, keepdims=True)
    spread = jnp.mean(center * center, axis=-1, keepdims=True)
    return center * lax.rsqrt(spread + 1e-06)


def gelu_tanh(value):
    return jax.nn.gelu(value, approximate=True)


def onehot_sum(select, values):
    upper = values.astype(BF16)
    lower = (values - upper.astype(F32)).astype(BF16)
    first = jnp.einsum("tl,tm->lm", select, upper, preferred_element_type=F32)
    return first + jnp.einsum("tl,tm->lm", select, lower, preferred_element_type=F32)


def on_device(
    tokens,
    condition,
    latent_lengths,
    in_weight,
    in_bias,
    out_weight,
    out_bias,
    up_weight,
    up_bias,
    down_weight,
    down_bias,
    mod_weight,
    mod_bias,
    out_grad,
):
    rows, width = tokens.shape
    latents = condition.shape[0]
    local_width = in_weight.shape[2]
    heads = local_width // HD
    data_size = lax.axis_size("dp")
    data_index = lax.axis_index("dp")
    tensor_index = lax.axis_index("tensor")
    quarter = rows // 4
    row_start = tensor_index * quarter

    def mine(value):
        return lax.dynamic_slice_in_dim(value, row_start, quarter, 0)

    places = jnp.arange(latents, dtype=jnp.int32)
    earlier = places[None, :] < places[:, None]
    starts = jnp.sum(jnp.where(earlier, latent_lengths[None, :], 0), axis=1)
    ends = starts + latent_lengths
    first_row = data_index * rows
    own_places = first_row + jnp.arange(rows, dtype=jnp.int32)

    def span_of(at):
        inside = (at[:, None] >= starts[None, :]) & (at[:, None] < ends[None, :])
        begin = jnp.sum(jnp.where(inside, starts[None, :] - first_row, 0), axis=1)
        end = jnp.sum(jnp.where(inside, ends[None, :] - first_row, 0), axis=1)
        return begin, end, inside

    begin, end, matches = span_of(own_places)
    select = matches.astype(BF16)
    select_mine = mine(select)
    span = jnp.stack([begin, end])
    bases = (-rows, 0, rows)
    forward_bounds = []
    backward_bounds = []
    for base in bases:
        low = jnp.clip(begin[::BQ] - base, 0, rows) // BK
        high = (jnp.clip(end[BQ - 1 :: BQ] - base, 0, rows) + BK - 1) // BK
        forward_bounds.append(jnp.stack([low, high]))
        key_at = first_row + base + jnp.arange(rows // BK, dtype=jnp.int32) * BK
        low = jnp.clip(span_of(key_at)[0], 0, rows) // BQ
        high = (jnp.clip(span_of(key_at + BK - 1)[1], 0, rows) + BQ - 1) // BQ
        valid = (key_at >= 0) & (key_at < rows * data_size)
        backward_bounds.append(jnp.where(valid[None, :], jnp.stack([low, high]), 0))
    forward_bounds = jnp.stack(forward_bounds)
    backward_bounds = jnp.stack(backward_bounds)

    cond_full = condition.astype(F32)
    silu_cond = jax.nn.silu(cond_full).astype(BF16)
    mod_local = (
        jnp.dot(silu_cond, mod_weight, preferred_element_type=F32) + mod_bias.astype(F32)
    ).astype(BF16)
    modulation = gather_tensor(mod_local[None])
    modulation = modulation.transpose(1, 0, 2).reshape(latents, 6 * width)

    def spread(chosen, first, count):
        return jnp.dot(
            chosen,
            modulation[:, first * width : (first + count) * width],
            preferred_element_type=BF16,
        )

    shift_scale = spread(select, 0, 2)
    shift_a = shift_scale[:, :width].astype(F32)
    scale_a = shift_scale[:, width:].astype(F32)
    others = spread(select_mine, 2, 4).astype(F32)
    gate_a, shift_m, scale_m, gate_m = (others[:, i * width : (i + 1) * width] for i in range(4))
    gate_m_all = spread(select, 5, 1).astype(F32)

    tokens_full = tokens.astype(F32)
    normed, norm_back = jax.vjp(layer_norm, tokens_full)
    entry = (normed * (1.0 + scale_a) + shift_a).astype(BF16)
    bias_full = in_bias.astype(F32)

    def project(which, bias):
        found = lax.dot_general(
            in_weight[:, which], entry, (((0,), (1,)), ((), ())), preferred_element_type=F32
        )
        if bias is not None:
            found = found + bias[:, None]
        return found.astype(BF16)

    keys = project(1, None)
    values = project(2, bias_full[1])
    pair = jnp.stack([keys, values])
    behind = shift(pair, "dp", 1)
    ahead = shift(pair, "dp", -1)
    query = project(0, bias_full[0]).reshape(heads, HD, rows)
    all_pairs = [p.reshape(2, heads, HD, rows) for p in (behind, pair, ahead)]
    all_keys = [p[0] for p in all_pairs]
    all_values = [p[1] for p in all_pairs]
    attended, logsum = attend(forward_bounds, span, query, all_keys, all_values, bases)
    attended_flat = attended.reshape(local_width, rows)
    attn_part = lax.dot_general(
        attended_flat, out_weight, (((0,), (1,)), ((), ())), preferred_element_type=F32
    )
    branch = scatter_tensor(attn_part) + out_bias.astype(F32)

    middle = mine(tokens).astype(F32) + gate_a * branch
    normed_m, norm_back_m = jax.vjp(layer_norm, middle)
    entry_m = gather_tensor((normed_m * (1.0 + scale_m) + shift_m).astype(BF16))
    hidden_pre = jnp.dot(entry_m, up_weight, preferred_element_type=F32) + up_bias.astype(F32)
    hidden_full, gelu_back = jax.vjp(gelu_tanh, hidden_pre)
    hidden = hidden_full.astype(BF16)
    grad_out = out_grad.astype(F32)
    grad_branch_m = (gate_m_all * grad_out).astype(BF16)
    grad_hidden = jnp.einsum("td,df->tf", grad_branch_m, down_weight, preferred_element_type=F32)
    grad_pre = gelu_back(grad_hidden)[0].astype(BF16)
    entry_part = jnp.einsum("tf,df->td", grad_pre, up_weight, preferred_element_type=F32)
    grad_entry_m = scatter_tensor(entry_part)
    mlp_part = jnp.einsum("tf,df->td", hidden, down_weight, preferred_element_type=F32)
    branch_m = scatter_tensor(mlp_part) + down_bias.astype(F32)
    output = (middle + gate_m * branch_m).astype(BF16)
    grad_out_mine = mine(out_grad).astype(F32)
    grad_gate_m = grad_out_mine * branch_m
    grad_down_b = jnp.sum(grad_branch_m.astype(F32), axis=0)
    grad_down_w = jnp.einsum("td,tf->df", grad_branch_m, hidden, preferred_element_type=F32)
    grad_up_b = jnp.sum(grad_pre.astype(F32), axis=0)
    grad_up_w = jnp.einsum("td,tf->df", entry_m, grad_pre, preferred_element_type=F32)
    grad_middle = grad_out_mine + norm_back_m(grad_entry_m * (1.0 + scale_m))[0]
    grad_gate_a = grad_middle * branch
    grad_branch_mine = (gate_a * grad_middle).astype(BF16)
    grad_out_b = jnp.sum(grad_branch_mine.astype(F32), axis=0)
    grad_branch = gather_tensor(grad_branch_mine)
    grad_attended = lax.dot_general(
        out_weight, grad_branch, (((0,), (1,)), ((), ())), preferred_element_type=F32
    ).astype(BF16)

    grad_query, grad_keys, grad_values = attend_back(
        backward_bounds,
        span,
        query,
        grad_attended.reshape(heads, HD, rows),
        attended,
        logsum,
        all_keys,
        all_values,
        bases,
    )
    to_behind = shift(jnp.stack([grad_keys[0], grad_values[0]]), "dp", -1)
    to_ahead = shift(jnp.stack([grad_keys[2], grad_values[2]]), "dp", 1)
    grad_out_w = lax.dot_general(
        grad_branch, attended_flat, (((0,), (1,)), ((), ())), preferred_element_type=F32
    )
    grad_kv = [
        (
            own[1].astype(F32) + to_behind[c].astype(F32) + to_ahead[c].astype(F32)
        ).astype(BF16).reshape(local_width, rows)
        for c, own in enumerate((grad_keys, grad_values))
    ]
    grad_proj = jnp.stack([grad_query.reshape(local_width, rows), *grad_kv])
    grad_in_w = jnp.einsum("td,cft->dcf", entry, grad_proj, preferred_element_type=F32)
    grad_in_b = jnp.stack(
        [jnp.sum(grad_proj[c].astype(F32), axis=1) for c in (0, 2)]
    )
    grad_entry = jnp.einsum("cft,dcf->td", grad_proj, in_weight, preferred_element_type=F32)
    input_part = norm_back(grad_entry * (1.0 + scale_a))[0]

    split_terms = jnp.concatenate([grad_entry, grad_entry * normed], axis=1)
    kept_terms = jnp.concatenate(
        [grad_gate_a, grad_entry_m, grad_entry_m * normed_m, grad_gate_m], axis=1
    )
    per_latent = jnp.concatenate(
        [onehot_sum(select, split_terms), onehot_sum(select_mine, kept_terms)], axis=1
    )
    columns_here = mod_weight.shape[1]
    arranged = per_latent.reshape(latents, 4, columns_here).transpose(1, 0, 2)
    grad_mod = lax.dynamic_index_in_dim(arranged, tensor_index, 0, keepdims=False)
    for bit in (1, 2, 3):
        grad_mod = grad_mod + swap(
            lax.dynamic_index_in_dim(arranged, tensor_index ^ bit, 0, keepdims=False), "tensor", bit
        )
    grad_mod = sum_all(grad_mod, "dp").astype(BF16)
    own_width = width // data_size
    own_silu = lax.dynamic_slice_in_dim(silu_cond, data_index * own_width, own_width, 1)
    grad_mod_w = jnp.einsum("ld,lm->dm", own_silu, grad_mod, preferred_element_type=F32)
    grad_mod_b = jnp.sum(grad_mod.astype(F32), axis=0)
    own_count = latents // data_size
    own_grad_mod = lax.dynamic_slice_in_dim(grad_mod, data_index * own_count, own_count, 0)
    own_cond = lax.dynamic_slice_in_dim(cond_full, data_index * own_count, own_count, 0)
    silu_grad = jnp.einsum("lm,dm->ld", own_grad_mod, mod_weight, preferred_element_type=F32)
    cond_part = jax.vjp(jax.nn.silu, own_cond)[1](silu_grad)[0]
    cond_parts = cond_part.reshape(own_count, 4, width // 4).transpose(1, 0, 2)
    grad_cond = lax.dynamic_index_in_dim(cond_parts, tensor_index, 0, keepdims=False)
    for bit in (1, 2, 3):
        grad_cond = grad_cond + swap(
            lax.dynamic_index_in_dim(cond_parts, tensor_index ^ bit, 0, keepdims=False),
            "tensor",
            bit,
        )

    placed = lax.dynamic_update_slice_in_dim(
        jnp.zeros((rows, width), F32), grad_middle, row_start, 0
    )
    grad_tokens = scatter_tensor((input_part + placed).T).T
    all_out_b = sum_all(grad_out_b, "tensor")
    small = jnp.concatenate([grad_in_b.reshape(-1), all_out_b, grad_up_b, grad_down_b])
    small = sum_all(small, "dp")
    cuts = [2 * local_width, 2 * local_width + width, 2 * local_width + width + grad_up_b.shape[0]]
    sum_in_b, sum_out_b, sum_up_b, sum_down_b = jnp.split(small, cuts)
    return (
        output,
        grad_tokens,
        grad_cond,
        scatter_data(grad_in_w),
        sum_in_b.reshape(2, local_width),
        scatter_data(grad_out_w),
        sum_out_b,
        scatter_data(grad_up_w),
        sum_up_b,
        scatter_data(grad_down_w),
        sum_down_b,
        grad_mod_w,
        grad_mod_b,
    )


def solution(mesh):
    placed = (
        P("dp", None),
        P(),
        P(),
        P(None, None, "tensor"),
        P(None, "tensor"),
        P(None, "tensor"),
        P(),
        P(None, "tensor"),
        P("tensor"),
        P(None, "tensor"),
        P(),
        P(None, "tensor"),
        P("tensor"),
        P("dp", None),
    )
    return jax.shard_map(
        on_device,
        mesh=mesh,
        in_specs=placed,
        out_specs=(
            P(("dp", "tensor"), None),
            P("dp", "tensor"),
            P("dp", "tensor"),
            P("dp", None, "tensor"),
            P(None, "tensor"),
            P("dp", "tensor"),
            P(),
            P("dp", "tensor"),
            P("tensor"),
            P("dp", "tensor"),
            P(),
            P("dp", "tensor"),
            P("tensor"),
        ),
        check_vma=False,
    )
```

time: 1380 us -> 524 us (0.38)
  waiting for transfers between devices: 715 us -> 155 us
  matrix products: 263 us -> 64.4 us
  starting transfers between devices: 15.4 us -> 151 us
  blocking collectives: 90.4 us -> 0 us
  other arithmetic: 146 us -> 61.1 us
  local copies, waits for them, and re-layouts: 115 us -> 35 us
  Pallas kernels: 0 us -> 46.9 us
    reduce_scatter x5 -> x0, waiting for transfers between devices: 511 us -> none  [the longest x1 151 us: on_device(): lax.psum_scatter(grad_mod_w, 'dp', scatter_dimension=0, tiled=True)]
    dot_general x33 -> x23, matrix products: 258 us -> 60.9 us  [the longest x1 7.99 us: on_device(): jnp.dot(entry_m, up_weight, preferred_element_type=F32)]
    ppermute x4 -> x60, starting transfers between devices: 14.2 us -> 151 us  [the longest x28 103 us: shift(): lax.ppermute(value, axis, [(i, i + distance) for i in devices if i + dist...]
    psum x2 -> x0, waiting for transfers between devices: 113 us -> none  [the longest x1 92.2 us: on_device(): lax.psum(entry_part.astype(jnp.bfloat16), 'tensor').astype(jnp.float32)]
    ppermute x4 -> x60, waiting for transfers between devices: 91 us -> 155 us  [the longest x28 90.6 us: shift(): lax.ppermute(value, axis, [(i, i + distance) for i in devices if i + dist...]
    convert_element_type x18 -> x15, other arithmetic: 64.1 us -> 16.1 us  [the longest x4 5.43 us: scatter_data(): half_low = half.astype(BF16)]
    unnamed x141 -> x182, local copies, waits for them, and re-layouts: 59.8 us -> 11.9 us
    pallas_call x0 -> x2, Pallas kernels: none -> 46.9 us  [the longest x1 23.6 us: attend(): pl.pallas_call(functools.partial(forward_kernel, bases, heads), out_shape...]
  transfers between devices with their start and end apart: 13 -> 60, of which waited for: 11 -> 18; matrix products, arithmetic and copies ran while one was open for 6% -> 18% of each run, Pallas kernels for 0% -> 5%
where the time goes in v1:
time: 524 us; the launch traced here: 517 us
  waiting for transfers between devices  155 us (30%)
  starting transfers between devices  151 us (29%)
  matrix products  64.4 us (12%)
  other arithmetic  61.1 us (12%)
  Pallas kernels  46.9 us (9%)
  local copies, waits for them, and re-layouts  35 us (7%)
    ppermute x28, starting transfers between devices, shift(): lax.ppermute(value, axis, [(i, i + distance) for i in devices if i + dist...  103 us
    ppermute x28, waiting for transfers between devices, shift(): lax.ppermute(value, axis, [(i, i + distance) for i in devices if i + dist...  90.6 us
    ppermute x32, waiting for transfers between devices, swap(): lax.ppermute(value, axis, [(i, i ^ bit) for i in range(lax.axis_size(axis...  64.6 us
    ppermute x32, starting transfers between devices, swap(): lax.ppermute(value, axis, [(i, i ^ bit) for i in range(lax.axis_size(axis...  47.6 us
    pallas_call x1, Pallas kernels, attend(): pl.pallas_call(functools.partial(forward_kernel, bases, heads), out_shape...  23.6 us
    pallas_call x1, Pallas kernels, attend_back(): pl.pallas_call(functools.partial(backward_kernel, bases, heads), out_shap...  23.3 us
    unnamed x182, local copies, waits for them, and re-layouts  11.9 us
    reduce_sum x4, other arithmetic, layer_norm(): center = value - jnp.mean(value, axis=-1, keepdims=True)  10.9 us
  transfers between devices with their start and end apart: 60, of which 18 were waited for; matrix products, arithmetic and copies ran while one was open for 18% of the time, Pallas kernels for 5%

profile of v1, /device:TPU:0, one launch (start us, length us, event | category | flops | bytes accessed | tf_op | source)
XLA Modules:
  0.0 516.6 jit_solution(14781137772229243930)
XLA Ops:
  1.5 3.3 fusion.25
  4.8 3.0 collective-permute-start
  24.8 5.8 %collective-permute-start.2 = (bf16[2,288,1024]{2,1,0:T(8,128)(2,1)}, bf16[2,288,1024]{2,1,0:T(8,128)(2,1)}, u32[]{:S(2)}, u32[]{:S(2)}) collective-permute-start(bf16[2,288,1024]{2,1,0:T(8,128)(2,1)} %pad_maximum_fusion.3), channel_id=1, source_target_pairs={{0,4},{4,8},{8,12},{12,16},{16,20},{20,24},{24,28},{1,5},{5,9},{9,... | collective-permute-start | bytes 3538952 | tf_op jit(solution)/shard_map/ppermute | solution.py:178
  33.4 19.7 %collective-permute-done.3 = bf16[2,288,1024]{2,1,0:T(8,128)(2,1)} collective-permute-done((bf16[2,288,1024]{2,1,0:T(8,128)(2,1)}, bf16[2,288,1024]{2,1,0:T(8,128)(2,1)}, u32[]{:S(2)}, u32[]{:S(2)}) %collective-permute-start.3) | collective-permute-done | bytes 1179680 | tf_op jit(solution)/shard_map/ppermute | solution.py:178
  54.5 23.9 %collective-permute-done.2 = bf16[2,288,1024]{2,1,0:T(8,128)(2,1)} collective-permute-done((bf16[2,288,1024]{2,1,0:T(8,128)(2,1)}, bf16[2,288,1024]{2,1,0:T(8,128)(2,1)}, u32[]{:S(2)}, u32[]{:S(2)}) %collective-permute-start.2) | collective-permute-done | bytes 1179680 | tf_op jit(solution)/shard_map/ppermute | solution.py:178
  79.8 23.6 %shard_map.237 = (bf16[4,72,1024]{2,1,0:T(8,128)(2,1)S(1)}, f32[4,1,1024]{2,1,0:T(1,128)S(1)}) custom-call(s32[3,2,4]{2,1,0:T(2,128)S(1)} %pad_add_fusion.1.bounds, s32[2,1024]{1,0:T(2,128)S(1)} %pad_add_fusion.span, bf16[4,72,1024]{2,1,0:T(8,128)(2,1)S(1)} %bitcast.443, bf16[4,72,1024]{2,1,0:T(8,128)(2,1)S(1)} %bitcast.437, ...), custom_call_target="tpu_custom_call" | custom-call | flops 7247757312 | bytes 12582912 | tf_op jit(solution)/shard_map/pallas_call | solution.py:77
  113.7 12.5 %collective-permute-done.5 = bf16[256,1152]{1,0:T(8,128)(2,1)} collective-permute-done((bf16[256,1152]{1,0:T(8,128)(2,1)}, bf16[256,1152]{1,0:T(8,128)(2,1)}, u32[]{:S(2)}, u32[]{:S(2)}) %collective-permute-start.5) | collective-permute-done | bytes 589856 | tf_op jit(solution)/shard_map/ppermute | solution.py:173
  129.7 13.3 %collective-permute-done.6 = bf16[256,1152]{1,0:T(8,128)(2,1)S(1)} collective-permute-done((bf16[256,1152]{1,0:T(8,128)(2,1)S(1)}, bf16[256,1152]{1,0:T(8,128)(2,1)S(1)}, u32[]{:S(2)}, u32[]{:S(2)}) %collective-permute-start.6) | collective-permute-done | bytes 589856 | tf_op jit(solution)/shard_map/ppermute | solution.py:173
  145.0 3.5 fusion.118
  149.5 8.0 %convert_reduce_fusion.2 = (f32[1152]{0:T(1024)}, bf16[1024,1152]{1,0:T(8,128)(2,1)S(1)}, f32[1024,1152]{1,0:T(8,128)}) fusion(f32[1024,1152]{1,0:T(8,128)S(1)} %fusion.118, f32[1152]{0:T(1024)S(1)} %copy-done.65, bf16[1024,1152]{1,0:T(8,128)(2,1)S(1)} %bitcast.475, bf16[1152,1152]{1,0:T(8,128)(2,1)S(1)} %copy-done), kind=kOutput, calls=%fused_computation.32 | convolution fusion | flops 2745039872 | bytes 16819200 | tf_op jit(solution)/shard_map/dot_general | solution.py:375
  157.5 5.9 %convolution_convert_fusion = bf16[1152,1152]{1,0:T(8,128)(2,1)S(1)} fusion(bf16[1024,1152]{1,0:T(8,128)(2,1)S(1)} %get-tuple-element.127, f32[1024,1152]{1,0:T(8,128)} %get-tuple-element.123), kind=kOutput, calls=%fused_computation.3 | convolution fusion | flops 2729852928 | bytes 9732096 | tf_op jit(solution)/shard_map/td,tf->df/dot_general | solution.py:390
  163.3 4.5 convolution_convert_fusion.5
  167.9 4.0 convolution_convert_fusion.4
  172.6 3.3 convolution_convert_fusion.1
  176.1 6.3 %collective-permute-start.46 = (bf16[4,144,1152]{2,1,0:T(8,128)(2,1)S(1)}, bf16[4,144,1152]{2,1,0:T(8,128)(2,1)S(1)}, u32[]{:S(2)}, u32[]{:S(2)}) collective-permute-start(bf16[4,144,1152]{2,1,0:T(8,128)(2,1)S(1)} %dynamic-slice_bitcast_fusion.1), channel_id=1, source_target_pairs={{0,4},{4,0},{8,12},{12,8},{16,20},{20,16},{24,28},{28,24},{1,5},{5... | collective-permute-start | bytes 3981320 | tf_op jit(solution)/shard_map/ppermute | solution.py:173
  185.4 27.0 %collective-permute-done.46 = bf16[4,144,1152]{2,1,0:T(8,128)(2,1)S(1)} collective-permute-done((bf16[4,144,1152]{2,1,0:T(8,128)(2,1)S(1)}, bf16[4,144,1152]{2,1,0:T(8,128)(2,1)S(1)}, u32[]{:S(2)}, u32[]{:S(2)}) %collective-permute-start.46) | collective-permute-done | bytes 1327136 | tf_op jit(solution)/shard_map/ppermute | solution.py:173
  215.2 7.3 %collective-permute-start.47 = (bf16[144,1152]{1,0:T(8,128)(2,1)S(1)}, bf16[144,1152]{1,0:T(8,128)(2,1)S(1)}, u32[]{:S(2)}, u32[]{:S(2)}) collective-permute-start(bf16[144,1152]{1,0:T(8,128)(2,1)S(1)} %get-tuple-element.83), channel_id=1, source_target_pairs={{0,8},{4,12},{8,16},{12,20},{16,24},{20,28},{1,9},{5,13},{9,17},{1... | collective-permute-start | bytes 995336 | tf_op jit(solution)/shard_map/ppermute | solution.py:178
  223.8 6.4 %collective-permute-start.51 = (bf16[144,1152]{1,0:T(8,128)(2,1)S(1)}, bf16[144,1152]{1,0:T(8,128)(2,1)S(1)}, u32[]{:S(2)}, u32[]{:S(2)}) collective-permute-start(bf16[144,1152]{1,0:T(8,128)(2,1)S(1)} %get-tuple-element.85), channel_id=1, source_target_pairs={{0,24},{4,28},{1,25},{5,29},{2,26},{6,30},{3,27},{7,31}} | collective-permute-start | bytes 995336 | tf_op jit(solution)/shard_map/ppermute | solution.py:178
  235.2 3.0 convert_reduce_fusion.3
  244.2 10.1 %collective-permute-start.49 = (bf16[144,1152]{1,0:T(8,128)(2,1)}, bf16[144,1152]{1,0:T(8,128)(2,1)}, u32[]{:S(2)}, u32[]{:S(2)}) collective-permute-start(bf16[144,1152]{1,0:T(8,128)(2,1)} %get-tuple-element.87), channel_id=1, source_target_pairs={{0,16},{4,20},{8,24},{12,28},{1,17},{5,21},{9,25},{13,29},{2,18},{... | collective-permute-start | bytes 995336 | tf_op jit(solution)/shard_map/ppermute | solution.py:178
  255.6 5.3 %collective-permute-start.54 = (bf16[144,1152]{1,0:T(8,128)(2,1)}, bf16[144,1152]{1,0:T(8,128)(2,1)}, u32[]{:S(2)}, u32[]{:S(2)}) collective-permute-start(bf16[144,1152]{1,0:T(8,128)(2,1)} %get-tuple-element.77), channel_id=1, source_target_pairs={{0,8},{4,12},{8,16},{12,20},{16,24},{20,28},{1,9},{5,13},{9,17},{1... | collective-permute-start | bytes 995336 | tf_op jit(solution)/shard_map/ppermute | solution.py:178
  263.9 7.1 %collective-permute-start.58 = (bf16[144,1152]{1,0:T(8,128)(2,1)S(1)}, bf16[144,1152]{1,0:T(8,128)(2,1)S(1)}, u32[]{:S(2)}, u32[]{:S(2)}) collective-permute-start(bf16[144,1152]{1,0:T(8,128)(2,1)S(1)} %copy-done.52), channel_id=1, source_target_pairs={{0,24},{4,28},{1,25},{5,29},{2,26},{6,30},{3,27},{7,31}} | collective-permute-start | bytes 995336 | tf_op jit(solution)/shard_map/ppermute | solution.py:178
  272.3 5.5 %collective-permute-start.56 = (bf16[144,1152]{1,0:T(8,128)(2,1)S(1)}, bf16[144,1152]{1,0:T(8,128)(2,1)S(1)}, u32[]{:S(2)}, u32[]{:S(2)}) collective-permute-start(bf16[144,1152]{1,0:T(8,128)(2,1)S(1)} %copy-done.50), channel_id=1, source_target_pairs={{0,16},{4,20},{8,24},{12,28},{1,17},{5,21},{9,25},{13,29},{2,18},{... | collective-permute-start | bytes 995336 | tf_op jit(solution)/shard_map/ppermute | solution.py:178
  282.0 5.3 %collective-permute-done.57 = bf16[144,1152]{1,0:T(8,128)(2,1)S(1)} collective-permute-done((bf16[144,1152]{1,0:T(8,128)(2,1)S(1)}, bf16[144,1152]{1,0:T(8,128)(2,1)S(1)}, u32[]{:S(2)}, u32[]{:S(2)}) %collective-permute-start.57) | collective-permute-done | bytes 331808 | tf_op jit(solution)/shard_map/ppermute | solution.py:178
  287.3 7.6 %collective-permute-done.55 = bf16[144,1152]{1,0:T(8,128)(2,1)S(1)} collective-permute-done((bf16[144,1152]{1,0:T(8,128)(2,1)S(1)}, bf16[144,1152]{1,0:T(8,128)(2,1)S(1)}, u32[]{:S(2)}, u32[]{:S(2)}) %collective-permute-start.55) | collective-permute-done | bytes 331808 | tf_op jit(solution)/shard_map/ppermute | solution.py:178
  313.3 23.3 %shard_map.238 = (bf16[4,72,1024]{2,1,0:T(8,128)(2,1)S(1)}, bf16[4,72,1024]{2,1,0:T(8,128)(2,1)S(1)}, bf16[4,72,1024]{2,1,0:T(8,128)(2,1)S(1)}, bf16[4,72,1024]{...) custom-call(s32[3,2,4]{2,1,0:T(2,128)S(1)} %pad_add_fusion.2.bounds,, ...), custom_call_target="tpu_custom_call" | custom-call | flops 18119393280 | bytes 25165824 | tf_op jit(solution)/shard_map/pallas_call | solution.py:151
  337.8 7.0 %collective-permute-start.15 = (bf16[2,4,72,1024]{3,2,1,0:T(8,128)(2,1)}, bf16[2,4,72,1024]{3,2,1,0:T(8,128)(2,1)}, u32[]{:S(2)}, u32[]{:S(2)}) collective-permute-start(bf16[2,4,72,1024]{3,2,1,0:T(8,128)(2,1)} %pad_maximum_fusion.5), channel_id=1, source_target_pairs={{0,4},{4,8},{8,12},{12,16},{16,20},{20,24},{24,28},{1,5},{5,9},{9,... | collective-permute-start | bytes 3538952 | tf_op jit(solution)/shard_map/ppermute | solution.py:178
  349.5 9.1 %collective-permute-start.40 = (bf16[144,288]{1,0:T(8,128)(2,1)S(1)}, bf16[144,288]{1,0:T(8,128)(2,1)S(1)}, u32[]{:S(2)}, u32[]{:S(2)}) collective-permute-start(bf16[144,288]{1,0:T(8,128)(2,1)S(1)} %get-tuple-element.103), channel_id=1, source_target_pairs={{0,8},{4,12},{8,16},{12,20},{16,24},{20,28},{1,9},{5,13},{9,17},{1... | collective-permute-start | bytes 248840 | tf_op jit(solution)/shard_map/ppermute | solution.py:178
  359.9 6.5 %collective-permute-start.44 = (bf16[144,288]{1,0:T(8,128)(2,1)S(1)}, bf16[144,288]{1,0:T(8,128)(2,1)S(1)}, u32[]{:S(2)}, u32[]{:S(2)}) collective-permute-start(bf16[144,288]{1,0:T(8,128)(2,1)S(1)} %get-tuple-element.105), channel_id=1, source_target_pairs={{0,24},{4,28},{1,25},{5,29},{2,26},{6,30},{3,27},{7,31}} | collective-permute-start | bytes 248840 | tf_op jit(solution)/shard_map/ppermute | solution.py:178
  368.1 16.8 %collective-permute-done.45 = bf16[144,288]{1,0:T(8,128)(2,1)S(1)} collective-permute-done((bf16[144,288]{1,0:T(8,128)(2,1)S(1)}, bf16[144,288]{1,0:T(8,128)(2,1)S(1)}, u32[]{:S(2)}, u32[]{:S(2)}) %collective-permute-start.45) | collective-permute-done | bytes 82976 | tf_op jit(solution)/shard_map/ppermute | solution.py:178
  390.4 3.0 collective-permute-done.41
  397.7 5.6 %convolution_convert_fusion.6 = bf16[1152,3,288]{0,2,1:T(8,128)(2,1)} fusion(bf16[1024,1152]{1,0:T(8,128)(2,1)} %copy-done.38, bf16[1,288,1024]{2,1,0:T(8,128)(2,1)S(1)} %bitcast.483, bf16[1,288,1024]{2,1,0:T(8,128)(2,1)S(1)} %bitcast.485, bf16[1,288,1024]{2,1,0:T(8,128)(2,1)S(1)} %bitcast.423), kind=kOutput, calls=%fused_computation.44 | convolution fusion | flops 2044735488 | bytes 6119424 | tf_op jit(solution)/shard_map/td,cft->dcf/dot_general | solution.py:425
  403.3 5.5 %fusion.12 = (f32[1024]{0:T(1024)S(1)}, f32[1024,1152]{1,0:T(8,128)}) fusion(bf16[1024,1152]{1,0:T(8,128)(2,1)S(1)} %copy-done.25, f32[1024]{0:T(1024)S(1)} %broadcast_multiply_fusion, bf16[1024,2304]{1,0:T(8,128)(2,1)S(1)} %bitcast.451, bf16[1152,3,288]{0,2,1:T(8,128)(2,1)S(1)} %copy-done.80, bf16[1,288,1024]{2,1,0:T(8,128)(2,1)S(1)} %bitcast.484, ...), kind=kOutput, calls=%fused_computation.22 | convolution fusion | flops 2048457728 | bytes 13205504 | tf_op jit(solution)/shard_map/cft,dcf->td/dot_general | solution.py:429
  409.0 3.2 collective-permute-start.36
  412.2 4.2 copy.68
  416.5 3.7 dynamic-slice_convert_fusion
  421.4 5.2 %fusion.112 = (f32[1024]{0:T(1024)S(1)}, f32[1024,1152]{1,0:T(8,128)}, f32[1024,1152]{1,0:T(8,128)S(1)}) fusion(f32[1024]{0:T(1024)S(1)} %multiply_multiply_fusion.3, f32[1024]{0:T(1024)S(1)} %broadcast_multiply_fusion, bf16[1024,1152]{1,0:T(8,128)(2,1)S(1)} %copy-done.25, f32[1024]{0:T(1024)S(1)} %fusion.81, f32[1024,1152]{1,0:T(8,128)S(1)} %bitcast.449, ...), kind=kLoop, calls=%fused_computation.350 | loop fusion | flops 14154752 | bytes 18890752 | tf_op jit(solution)/shard_map/transpose(jvp())/reduce_sum | solution.py:244
  431.1 2.8 broadcast_add_fusion
  435.3 6.3 %collective-permute-start.37 = (f32[4032]{0:T(1024)S(1)}, f32[4032]{0:T(1024)S(1)}, u32[]{:S(2)}, u32[]{:S(2)}) collective-permute-start(f32[4032]{0:T(1024)S(1)} %add.810), channel_id=1, source_target_pairs={{0,8},{4,12},{8,0},{12,4},{16,24},{20,28},{24,16},{28,20},{1,9},{5... | collective-permute-start | bytes 48392 | tf_op jit(solution)/shard_map/ppermute | solution.py:173
  444.4 2.8 copy.67
  447.3 3.0 collective-permute-start.38
  450.3 3.0 collective-permute-done.21
  453.3 6.3 %collective-permute-start.22 = (f32[16,1728]{1,0:T(8,128)S(1)}, f32[16,1728]{1,0:T(8,128)S(1)}, u32[]{:S(2)}, u32[]{:S(2)}) collective-permute-start(f32[16,1728]{1,0:T(8,128)S(1)} %add.783), channel_id=1, source_target_pairs={{0,8},{4,12},{8,0},{12,4},{16,24},{20,28},{24,16},{28,20},{1,9},{5... | collective-permute-start | bytes 331784 | tf_op jit(solution)/shard_map/ppermute | solution.py:173
  462.4 4.7 collective-permute-start.23
  482.8 6.4 %collective-permute-start.32 = (bf16[144,3,288]{2,0,1:T(8,128)(2,1)S(1)}, bf16[144,3,288]{2,0,1:T(8,128)(2,1)S(1)}, u32[]{:S(2)}, u32[]{:S(2)}) collective-permute-start(bf16[144,3,288]{2,0,1:T(8,128)(2,1)S(1)} %get-tuple-element.91), channel_id=1, source_target_pairs={{0,24},{4,28},{1,25},{5,29},{2,26},{6,30},{3,27},{7,31}} | collective-permute-start | bytes 746504 | tf_op jit(solution)/shard_map/ppermute | solution.py:178
  490.6 5.5 %collective-permute-start.30 = (bf16[144,3,288]{2,0,1:T(8,128)(2,1)S(1)}, bf16[144,3,288]{2,0,1:T(8,128)(2,1)S(1)}, u32[]{:S(2)}, u32[]{:S(2)}) collective-permute-start(bf16[144,3,288]{2,0,1:T(8,128)(2,1)S(1)} %get-tuple-element.93), channel_id=1, source_target_pairs={{0,16},{4,20},{8,24},{12,28},{1,17},{5,21},{9,25},{13,29},{2,18},{... | collective-permute-start | bytes 746504 | tf_op jit(solution)/shard_map/ppermute | solution.py:178
  501.6 6.2 %collective-permute-done.31 = bf16[144,3,288]{2,0,1:T(8,128)(2,1)S(1)} collective-permute-done((bf16[144,3,288]{2,0,1:T(8,128)(2,1)S(1)}, bf16[144,3,288]{2,0,1:T(8,128)(2,1)S(1)}, u32[]{:S(2)}, u32[]{:S(2)}) %collective-permute-start.31) | collective-permute-done | bytes 248864 | tf_op jit(solution)/shard_map/ppermute | solution.py:178
  507.8 6.1 %collective-permute-done.29 = bf16[144,3,288]{2,0,1:T(8,128)(2,1)S(1)} collective-permute-done((bf16[144,3,288]{2,0,1:T(8,128)(2,1)S(1)}, bf16[144,3,288]{2,0,1:T(8,128)(2,1)S(1)}, u32[]{:S(2)}, u32[]{:S(2)}) %collective-permute-start.29) | collective-permute-done | bytes 248864 | tf_op jit(solution)/shard_map/ppermute | solution.py:178
  (416 shorter events, 142.5 us)
Async XLA Ops:
  22.9 30.2 %collective-permute-start.3 = (bf16[2,288,1024]{2,1,0:T(8,128)(2,1)}, bf16[2,288,1024]{2,1,0:T(8,128)(2,1)}, u32[]{:S(2)}, u32[]{:S(2)}) collective-permute-start(bf16[2,288,1024]{2,1,0:T(8,128)(2,1)} %pad_maximum_fusion.3), channel_id=1, source_target_pairs={{4,0},{8,4},{12,8},{16,12},{20,16},{24,20},{28,24},{5,1},{9,5},{13... | collective-permute-start | bytes 3538952 | tf_op jit(solution)/shard_map/ppermute | solution.py:178
  24.8 53.6 %collective-permute-start.2 = (bf16[2,288,1024]{2,1,0:T(8,128)(2,1)}, bf16[2,288,1024]{2,1,0:T(8,128)(2,1)}, u32[]{:S(2)}, u32[]{:S(2)}) collective-permute-start(bf16[2,288,1024]{2,1,0:T(8,128)(2,1)} %pad_maximum_fusion.3), channel_id=1, source_target_pairs={{0,4},{4,8},{8,12},{12,16},{16,20},{20,24},{24,28},{1,5},{5,9},{9,... | collective-permute-start | bytes 3538952 | tf_op jit(solution)/shard_map/ppermute | solution.py:178
  110.4 15.7 %collective-permute-start.5 = (bf16[256,1152]{1,0:T(8,128)(2,1)}, bf16[256,1152]{1,0:T(8,128)(2,1)}, u32[]{:S(2)}, u32[]{:S(2)}) collective-permute-start(bf16[256,1152]{1,0:T(8,128)(2,1)} %fusion.62), channel_id=1, source_target_pairs={{0,2},{1,3},{2,0},{3,1},{4,6},{5,7},{6,4},{7,5},{8,10},{9,11},{10,... | collective-permute-start | bytes 1769480 | tf_op jit(solution)/shard_map/ppermute | solution.py:173
  128.5 14.6 %collective-permute-start.6 = (bf16[256,1152]{1,0:T(8,128)(2,1)S(1)}, bf16[256,1152]{1,0:T(8,128)(2,1)S(1)}, u32[]{:S(2)}, u32[]{:S(2)}) collective-permute-start(bf16[256,1152]{1,0:T(8,128)(2,1)S(1)} %fusion.31), channel_id=1, source_target_pairs={{0,2},{1,3},{2,0},{3,1},{4,6},{5,7},{6,4},{7,5},{8,10},{9,11},{10,... | collective-permute-start | bytes 1769480 | tf_op jit(solution)/shard_map/ppermute | solution.py:173
  176.1 36.3 %collective-permute-start.46 = (bf16[4,144,1152]{2,1,0:T(8,128)(2,1)S(1)}, bf16[4,144,1152]{2,1,0:T(8,128)(2,1)S(1)}, u32[]{:S(2)}, u32[]{:S(2)}) collective-permute-start(bf16[4,144,1152]{2,1,0:T(8,128)(2,1)S(1)} %dynamic-slice_bitcast_fusion.1), channel_id=1, source_target_pairs={{0,4},{4,0},{8,12},{12,8},{16,20},{20,16},{24,28},{28,24},{1,5},{5... | collective-permute-start | bytes 3981320 | tf_op jit(solution)/shard_map/ppermute | solution.py:173
  182.5 58.0 %collective-permute-start.53 = (bf16[4,144,1152]{2,1,0:T(8,128)(2,1)S(1)}, bf16[4,144,1152]{2,1,0:T(8,128)(2,1)S(1)}, u32[]{:S(2)}, u32[]{:S(2)}) collective-permute-start(bf16[4,144,1152]{2,1,0:T(8,128)(2,1)S(1)} %dynamic-slice_bitcast_fusion), channel_id=1, source_target_pairs={{0,4},{4,0},{8,12},{12,8},{16,20},{20,16},{24,28},{28,24},{1,5},{5... | collective-permute-start | bytes 3981320 | tf_op jit(solution)/shard_map/ppermute | solution.py:173
  182.9 40.9 %collective-permute-start.11 = (bf16[256,1152]{1,0:T(8,128)(2,1)S(1)}, bf16[256,1152]{1,0:T(8,128)(2,1)S(1)}, u32[]{:S(2)}, u32[]{:S(2)}) collective-permute-start(bf16[256,1152]{1,0:T(8,128)(2,1)S(1)} %fusion.64), channel_id=1, source_target_pairs={{0,2},{1,3},{2,0},{3,1},{4,6},{5,7},{6,4},{7,5},{8,10},{9,11},{10,... | collective-permute-start | bytes 1769480 | tf_op jit(solution)/shard_map/ppermute | solution.py:173
  183.9 48.0 %collective-permute-start.9 = (bf16[256,1152]{1,0:T(8,128)(2,1)S(1)}, bf16[256,1152]{1,0:T(8,128)(2,1)S(1)}, u32[]{:S(2)}, u32[]{:S(2)}) collective-permute-start(bf16[256,1152]{1,0:T(8,128)(2,1)S(1)} %fusion.63), channel_id=1, source_target_pairs={{0,2},{1,3},{2,0},{3,1},{4,6},{5,7},{6,4},{7,5},{8,10},{9,11},{10,... | collective-permute-start | bytes 1769480 | tf_op jit(solution)/shard_map/ppermute | solution.py:173
  215.2 29.0 %collective-permute-start.47 = (bf16[144,1152]{1,0:T(8,128)(2,1)S(1)}, bf16[144,1152]{1,0:T(8,128)(2,1)S(1)}, u32[]{:S(2)}, u32[]{:S(2)}) collective-permute-start(bf16[144,1152]{1,0:T(8,128)(2,1)S(1)} %get-tuple-element.83), channel_id=1, source_target_pairs={{0,8},{4,12},{8,16},{12,20},{16,24},{20,28},{1,9},{5,13},{9,17},{1... | collective-permute-start | bytes 995336 | tf_op jit(solution)/shard_map/ppermute | solution.py:178
  222.5 31.8 %collective-permute-start.52 = (bf16[144,1152]{1,0:T(8,128)(2,1)S(1)}, bf16[144,1152]{1,0:T(8,128)(2,1)S(1)}, u32[]{:S(2)}, u32[]{:S(2)}) collective-permute-start(bf16[144,1152]{1,0:T(8,128)(2,1)S(1)} %get-tuple-element.84), channel_id=1, source_target_pairs={{24,0},{28,4},{25,1},{29,5},{26,2},{30,6},{27,3},{31,7}} | collective-permute-start | bytes 995336 | tf_op jit(solution)/shard_map/ppermute | solution.py:178
  223.8 31.8 %collective-permute-start.51 = (bf16[144,1152]{1,0:T(8,128)(2,1)S(1)}, bf16[144,1152]{1,0:T(8,128)(2,1)S(1)}, u32[]{:S(2)}, u32[]{:S(2)}) collective-permute-start(bf16[144,1152]{1,0:T(8,128)(2,1)S(1)} %get-tuple-element.85), channel_id=1, source_target_pairs={{0,24},{4,28},{1,25},{5,29},{2,26},{6,30},{3,27},{7,31}} | collective-permute-start | bytes 995336 | tf_op jit(solution)/shard_map/ppermute | solution.py:178
  231.9 31.3 %collective-permute-start.50 = (bf16[144,1152]{1,0:T(8,128)(2,1)}, bf16[144,1152]{1,0:T(8,128)(2,1)}, u32[]{:S(2)}, u32[]{:S(2)}) collective-permute-start(bf16[144,1152]{1,0:T(8,128)(2,1)} %get-tuple-element.86), channel_id=1, source_target_pairs={{16,0},{20,4},{24,8},{28,12},{17,1},{21,5},{25,9},{29,13},{18,2},{... | collective-permute-start | bytes 995336 | tf_op jit(solution)/shard_map/ppermute | solution.py:178
  240.5 20.4 %collective-permute-start.12 = (bf16[256,1152]{1,0:T(8,128)(2,1)S(1)}, bf16[256,1152]{1,0:T(8,128)(2,1)S(1)}, u32[]{:S(2)}, u32[]{:S(2)}) collective-permute-start(bf16[256,1152]{1,0:T(8,128)(2,1)S(1)} %get-tuple-element.55), channel_id=1, source_target_pairs={{0,2},{1,3},{2,0},{3,1},{4,6},{5,7},{6,4},{7,5},{8,10},{9,11},{10,... | collective-permute-start | bytes 1769480 | tf_op jit(solution)/shard_map/ppermute | solution.py:173
  244.2 26.8 %collective-permute-start.49 = (bf16[144,1152]{1,0:T(8,128)(2,1)}, bf16[144,1152]{1,0:T(8,128)(2,1)}, u32[]{:S(2)}, u32[]{:S(2)}) collective-permute-start(bf16[144,1152]{1,0:T(8,128)(2,1)} %get-tuple-element.87), channel_id=1, source_target_pairs={{0,16},{4,20},{8,24},{12,28},{1,17},{5,21},{9,25},{13,29},{2,18},{... | collective-permute-start | bytes 995336 | tf_op jit(solution)/shard_map/ppermute | solution.py:178
  254.3 18.0 %collective-permute-start.48 = (bf16[144,1152]{1,0:T(8,128)(2,1)}, bf16[144,1152]{1,0:T(8,128)(2,1)}, u32[]{:S(2)}, u32[]{:S(2)}) collective-permute-start(bf16[144,1152]{1,0:T(8,128)(2,1)} %get-tuple-element.88), channel_id=1, source_target_pairs={{8,0},{12,4},{16,8},{20,12},{24,16},{28,20},{9,1},{13,5},{17,9},{2... | collective-permute-start | bytes 995336 | tf_op jit(solution)/shard_map/ppermute | solution.py:178
  255.6 22.2 %collective-permute-start.54 = (bf16[144,1152]{1,0:T(8,128)(2,1)}, bf16[144,1152]{1,0:T(8,128)(2,1)}, u32[]{:S(2)}, u32[]{:S(2)}) collective-permute-start(bf16[144,1152]{1,0:T(8,128)(2,1)} %get-tuple-element.77), channel_id=1, source_target_pairs={{0,8},{4,12},{8,16},{12,20},{16,24},{20,28},{1,9},{5,13},{9,17},{1... | collective-permute-start | bytes 995336 | tf_op jit(solution)/shard_map/ppermute | solution.py:178
  260.9 18.4 %collective-permute-start.59 = (bf16[144,1152]{1,0:T(8,128)(2,1)}, bf16[144,1152]{1,0:T(8,128)(2,1)}, u32[]{:S(2)}, u32[]{:S(2)}) collective-permute-start(bf16[144,1152]{1,0:T(8,128)(2,1)} %get-tuple-element.78), channel_id=1, source_target_pairs={{24,0},{28,4},{25,1},{29,5},{26,2},{30,6},{27,3},{31,7}} | collective-permute-start | bytes 995336 | tf_op jit(solution)/shard_map/ppermute | solution.py:178
  263.9 18.1 %collective-permute-start.58 = (bf16[144,1152]{1,0:T(8,128)(2,1)S(1)}, bf16[144,1152]{1,0:T(8,128)(2,1)S(1)}, u32[]{:S(2)}, u32[]{:S(2)}) collective-permute-start(bf16[144,1152]{1,0:T(8,128)(2,1)S(1)} %copy-done.52), channel_id=1, source_target_pairs={{0,24},{4,28},{1,25},{5,29},{2,26},{6,30},{3,27},{7,31}} | collective-permute-start | bytes 995336 | tf_op jit(solution)/shard_map/ppermute | solution.py:178
  271.0 16.3 %collective-permute-start.57 = (bf16[144,1152]{1,0:T(8,128)(2,1)S(1)}, bf16[144,1152]{1,0:T(8,128)(2,1)S(1)}, u32[]{:S(2)}, u32[]{:S(2)}) collective-permute-start(bf16[144,1152]{1,0:T(8,128)(2,1)S(1)} %copy-done.51), channel_id=1, source_target_pairs={{16,0},{20,4},{24,8},{28,12},{17,1},{21,5},{25,9},{29,13},{18,2},{... | collective-permute-start | bytes 995336 | tf_op jit(solution)/shard_map/ppermute | solution.py:178
  272.3 15.0 %collective-permute-start.56 = (bf16[144,1152]{1,0:T(8,128)(2,1)S(1)}, bf16[144,1152]{1,0:T(8,128)(2,1)S(1)}, u32[]{:S(2)}, u32[]{:S(2)}) collective-permute-start(bf16[144,1152]{1,0:T(8,128)(2,1)S(1)} %copy-done.50), channel_id=1, source_target_pairs={{0,16},{4,20},{8,24},{12,28},{1,17},{5,21},{9,25},{13,29},{2,18},{... | collective-permute-start | bytes 995336 | tf_op jit(solution)/shard_map/ppermute | solution.py:178
  277.9 17.0 %collective-permute-start.55 = (bf16[144,1152]{1,0:T(8,128)(2,1)S(1)}, bf16[144,1152]{1,0:T(8,128)(2,1)S(1)}, u32[]{:S(2)}, u32[]{:S(2)}) collective-permute-start(bf16[144,1152]{1,0:T(8,128)(2,1)S(1)} %copy-done.49), channel_id=1, source_target_pairs={{8,0},{12,4},{16,8},{20,12},{24,16},{28,20},{9,1},{13,5},{17,9},{2... | collective-permute-start | bytes 995336 | tf_op jit(solution)/shard_map/ppermute | solution.py:178
  279.4 18.1 %collective-permute-start.13 = (bf16[2,256,1152]{2,1,0:T(8,128)(2,1)S(1)}, bf16[2,256,1152]{2,1,0:T(8,128)(2,1)S(1)}, u32[]{:S(2)}, u32[]{:S(2)}) collective-permute-start(bf16[2,256,1152]{2,1,0:T(8,128)(2,1)S(1)} %maximum_select_fusion.3), channel_id=1, source_target_pairs={{0,1},{1,0},{2,3},{3,2},{4,5},{5,4},{6,7},{7,6},{8,9},{9,8},{10,11... | collective-permute-start | bytes 3538952 | tf_op jit(solution)/shard_map/ppermute | solution.py:173
  297.3 50.4 %collective-permute-start.34 = (f32[1152]{0:T(1024)S(1)}, f32[1152]{0:T(1024)S(1)}, u32[]{:S(2)}, u32[]{:S(2)}) collective-permute-start(f32[1152]{0:T(1024)S(1)} %get-tuple-element.54), channel_id=1, source_target_pairs={{0,1},{1,0},{2,3},{3,2},{4,5},{5,4},{6,7},{7,6},{8,9},{9,8},{10,11... | collective-permute-start | bytes 13832 | tf_op jit(solution)/shard_map/ppermute | solution.py:173
  306.1 43.1 %collective-permute-start.39 = (bf16[4,144,288]{2,1,0:T(8,128)(2,1)S(1)}, bf16[4,144,288]{2,1,0:T(8,128)(2,1)S(1)}, u32[]{:S(2)}, u32[]{:S(2)}) collective-permute-start(bf16[4,144,288]{2,1,0:T(8,128)(2,1)S(1)} %dynamic-slice_bitcast_fusion.6), channel_id=1, source_target_pairs={{0,4},{4,0},{8,12},{12,8},{16,20},{20,16},{24,28},{28,24},{1,5},{5... | collective-permute-start | bytes 995336 | tf_op jit(solution)/shard_map/ppermute | solution.py:173
  337.8 57.7 %collective-permute-start.15 = (bf16[2,4,72,1024]{3,2,1,0:T(8,128)(2,1)}, bf16[2,4,72,1024]{3,2,1,0:T(8,128)(2,1)}, u32[]{:S(2)}, u32[]{:S(2)}) collective-permute-start(bf16[2,4,72,1024]{3,2,1,0:T(8,128)(2,1)} %pad_maximum_fusion.5), channel_id=1, source_target_pairs={{0,4},{4,8},{8,12},{12,16},{16,20},{20,24},{24,28},{1,5},{5,9},{9,... | collective-permute-start | bytes 3538952 | tf_op jit(solution)/shard_map/ppermute | solution.py:178
  345.9 49.6 %collective-permute-start.14 = (bf16[2,4,72,1024]{3,2,1,0:T(8,128)(2,1)}, bf16[2,4,72,1024]{3,2,1,0:T(8,128)(2,1)}, u32[]{:S(2)}, u32[]{:S(2)}) collective-permute-start(bf16[2,4,72,1024]{3,2,1,0:T(8,128)(2,1)} %pad_maximum_fusion.4), channel_id=1, source_target_pairs={{4,0},{8,4},{12,8},{16,12},{20,16},{24,20},{28,24},{5,1},{9,5},{13... | collective-permute-start | bytes 3538952 | tf_op jit(solution)/shard_map/ppermute | solution.py:178
  347.7 12.1 %collective-permute-start.35 = (f32[1152]{0:T(1024)S(1)}, f32[1152]{0:T(1024)S(1)}, u32[]{:S(2)}, u32[]{:S(2)}) collective-permute-start(f32[1152]{0:T(1024)S(1)} %add.808), channel_id=1, source_target_pairs={{0,2},{1,3},{2,0},{3,1},{4,6},{5,7},{6,4},{7,5},{8,10},{9,11},{10,... | collective-permute-start | bytes 13832 | tf_op jit(solution)/shard_map/ppermute | solution.py:173
  349.5 17.4 %collective-permute-start.40 = (bf16[144,288]{1,0:T(8,128)(2,1)S(1)}, bf16[144,288]{1,0:T(8,128)(2,1)S(1)}, u32[]{:S(2)}, u32[]{:S(2)}) collective-permute-start(bf16[144,288]{1,0:T(8,128)(2,1)S(1)} %get-tuple-element.103), channel_id=1, source_target_pairs={{0,8},{4,12},{8,16},{12,20},{16,24},{20,28},{1,9},{5,13},{9,17},{1... | collective-permute-start | bytes 248840 | tf_op jit(solution)/shard_map/ppermute | solution.py:178
  358.6 26.3 %collective-permute-start.45 = (bf16[144,288]{1,0:T(8,128)(2,1)S(1)}, bf16[144,288]{1,0:T(8,128)(2,1)S(1)}, u32[]{:S(2)}, u32[]{:S(2)}) collective-permute-start(bf16[144,288]{1,0:T(8,128)(2,1)S(1)} %get-tuple-element.104), channel_id=1, source_target_pairs={{24,0},{28,4},{25,1},{29,5},{26,2},{30,6},{27,3},{31,7}} | collective-permute-start | bytes 248840 | tf_op jit(solution)/shard_map/ppermute | solution.py:178
  359.9 26.9 %collective-permute-start.44 = (bf16[144,288]{1,0:T(8,128)(2,1)S(1)}, bf16[144,288]{1,0:T(8,128)(2,1)S(1)}, u32[]{:S(2)}, u32[]{:S(2)}) collective-permute-start(bf16[144,288]{1,0:T(8,128)(2,1)S(1)} %get-tuple-element.105), channel_id=1, source_target_pairs={{0,24},{4,28},{1,25},{5,29},{2,26},{6,30},{3,27},{7,31}} | collective-permute-start | bytes 248840 | tf_op jit(solution)/shard_map/ppermute | solution.py:178
  366.8 23.6 %collective-permute-start.43 = (bf16[144,288]{1,0:T(8,128)(2,1)S(1)}, bf16[144,288]{1,0:T(8,128)(2,1)}, u32[]{:S(2)}, u32[]{:S(2)}) collective-permute-start(bf16[144,288]{1,0:T(8,128)(2,1)S(1)} %get-tuple-element.106), channel_id=1, source_target_pairs={{16,0},{20,4},{24,8},{28,12},{17,1},{21,5},{25,9},{29,13},{18,2},{... | collective-permute-start | bytes 248840 | tf_op jit(solution)/shard_map/ppermute | solution.py:178
  409.0 26.3 %collective-permute-start.36 = (f32[4032]{0:T(1024)S(1)}, f32[4032]{0:T(1024)S(1)}, u32[]{:S(2)}, u32[]{:S(2)}) collective-permute-start(f32[4032]{0:T(1024)S(1)} %concatenate.100), channel_id=1, source_target_pairs={{0,4},{4,0},{8,12},{12,8},{16,20},{20,16},{24,28},{28,24},{1,5},{5... | collective-permute-start | bytes 48392 | tf_op jit(solution)/shard_map/ppermute | solution.py:173
  421.4 54.9 %collective-permute-start.27 = (bf16[4,144,3,288]{3,1,2,0:T(8,128)(2,1)}, bf16[4,144,3,288]{3,1,2,0:T(8,128)(2,1)}, u32[]{:S(2)}, u32[]{:S(2)}) collective-permute-start(bf16[4,144,3,288]{3,1,2,0:T(8,128)(2,1)} %bitcast.415), channel_id=1, source_target_pairs={{0,4},{4,0},{8,12},{12,8},{16,20},{20,16},{24,28},{28,24},{1,5},{5... | collective-permute-start | bytes 2985992 | tf_op jit(solution)/shard_map/ppermute | solution.py:173
  429.1 12.6 %collective-permute-start.18 = (f32[16,1728]{1,0:T(8,128)S(1)}, f32[16,1728]{1,0:T(8,128)S(1)}, u32[]{:S(2)}, u32[]{:S(2)}) collective-permute-start(f32[16,1728]{1,0:T(8,128)S(1)} %bitcast.494), channel_id=1, source_target_pairs={{0,1},{1,0},{2,3},{3,2},{4,5},{5,4},{6,7},{7,6},{8,9},{9,8},{10,11... | collective-permute-start | bytes 331784 | tf_op jit(solution)/shard_map/ppermute | solution.py:173
  429.2 12.5 %collective-permute-start.19 = (f32[16,1728]{1,0:T(8,128)S(1)}, f32[16,1728]{1,0:T(8,128)S(1)}, u32[]{:S(2)}, u32[]{:S(2)}) collective-permute-start(f32[16,1728]{1,0:T(8,128)S(1)} %bitcast.493), channel_id=1, source_target_pairs={{0,2},{1,3},{2,0},{3,1},{4,6},{5,7},{6,4},{7,5},{8,10},{9,11},{10,... | collective-permute-start | bytes 331784 | tf_op jit(solution)/shard_map/ppermute | solution.py:173
  435.3 11.9 %collective-permute-start.37 = (f32[4032]{0:T(1024)S(1)}, f32[4032]{0:T(1024)S(1)}, u32[]{:S(2)}, u32[]{:S(2)}) collective-permute-start(f32[4032]{0:T(1024)S(1)} %add.810), channel_id=1, source_target_pairs={{0,8},{4,12},{8,0},{12,4},{16,24},{20,28},{24,16},{28,20},{1,9},{5... | collective-permute-start | bytes 48392 | tf_op jit(solution)/shard_map/ppermute | solution.py:173
  441.7 11.6 %collective-permute-start.21 = (f32[16,1728]{1,0:T(8,128)S(1)}, f32[16,1728]{1,0:T(8,128)S(1)}, u32[]{:S(2)}, u32[]{:S(2)}) collective-permute-start(f32[16,1728]{1,0:T(8,128)S(1)} %fusion.73), channel_id=1, source_target_pairs={{0,4},{4,0},{8,12},{12,8},{16,20},{20,16},{24,28},{28,24},{1,5},{5... | collective-permute-start | bytes 331784 | tf_op jit(solution)/shard_map/ppermute | solution.py:173
  447.3 13.4 %collective-permute-start.38 = (f32[4032]{0:T(1024)S(1)}, f32[4032]{0:T(1024)S(1)}, u32[]{:S(2)}, u32[]{:S(2)}) collective-permute-start(f32[4032]{0:T(1024)S(1)} %add.811), channel_id=1, source_target_pairs={{0,16},{4,20},{8,24},{12,28},{16,0},{20,4},{24,8},{28,12},{1,17},{... | collective-permute-start | bytes 48392 | tf_op jit(solution)/shard_map/ppermute | solution.py:173
  460.7 19.0 %collective-permute-start.16 = (bf16[2,288,1024]{2,1,0:T(8,128)(2,1)}, bf16[2,288,1024]{2,1,0:T(8,128)(2,1)}, u32[]{:S(2)}, u32[]{:S(2)}) collective-permute-start(bf16[2,288,1024]{2,1,0:T(8,128)(2,1)} %dynamic-slice_bitcast_fusion.2), channel_id=1, source_target_pairs={{0,1},{1,0},{2,3},{3,2},{4,5},{5,4},{6,7},{7,6},{8,9},{9,8},{10,11... | collective-permute-start | bytes 3538952 | tf_op jit(solution)/shard_map/ppermute | solution.py:173
  474.4 14.8 %collective-permute-start.25 = (f32[2,288]{1,0:T(2,128)S(1)}, f32[2,288]{1,0:T(2,128)S(1)}, u32[]{:S(2)}, u32[]{:S(2)}) collective-permute-start(f32[2,288]{1,0:T(2,128)S(1)} %bitcast.499), channel_id=1, source_target_pairs={{0,2},{1,3},{2,0},{3,1},{4,6},{5,7},{6,4},{7,5},{8,10},{9,11},{10,... | collective-permute-start | bytes 6920 | tf_op jit(solution)/shard_map/ppermute | solution.py:173
  476.0 14.6 %collective-permute-start.26 = (f32[2,288]{1,0:T(2,128)S(1)}, f32[2,288]{1,0:T(2,128)S(1)}, u32[]{:S(2)}, u32[]{:S(2)}) collective-permute-start(f32[2,288]{1,0:T(2,128)S(1)} %bitcast.498), channel_id=1, source_target_pairs={{0,3},{1,2},{2,1},{3,0},{4,7},{5,6},{6,5},{7,4},{8,11},{9,10},{10,... | collective-permute-start | bytes 6920 | tf_op jit(solution)/shard_map/ppermute | solution.py:173
  478.2 17.8 %collective-permute-start.28 = (bf16[144,3,288]{2,0,1:T(8,128)(2,1)S(1)}, bf16[144,3,288]{2,0,1:T(8,128)(2,1)S(1)}, u32[]{:S(2)}, u32[]{:S(2)}) collective-permute-start(bf16[144,3,288]{2,0,1:T(8,128)(2,1)S(1)} %get-tuple-element.89), channel_id=1, source_target_pairs={{0,8},{4,12},{8,16},{12,20},{16,24},{20,28},{1,9},{5,13},{9,17},{1... | collective-permute-start | bytes 746504 | tf_op jit(solution)/shard_map/ppermute | solution.py:178
  479.7 17.7 %collective-permute-start.33 = (bf16[144,3,288]{2,0,1:T(8,128)(2,1)S(1)}, bf16[144,3,288]{2,0,1:T(8,128)(2,1)S(1)}, u32[]{:S(2)}, u32[]{:S(2)}) collective-permute-start(bf16[144,3,288]{2,0,1:T(8,128)(2,1)S(1)} %get-tuple-element.90), channel_id=1, source_target_pairs={{24,0},{28,4},{25,1},{29,5},{26,2},{30,6},{27,3},{31,7}} | collective-permute-start | bytes 746504 | tf_op jit(solution)/shard_map/ppermute | solution.py:178
  482.8 18.7 %collective-permute-start.32 = (bf16[144,3,288]{2,0,1:T(8,128)(2,1)S(1)}, bf16[144,3,288]{2,0,1:T(8,128)(2,1)S(1)}, u32[]{:S(2)}, u32[]{:S(2)}) collective-permute-start(bf16[144,3,288]{2,0,1:T(8,128)(2,1)S(1)} %get-tuple-element.91), channel_id=1, source_target_pairs={{0,24},{4,28},{1,25},{5,29},{2,26},{6,30},{3,27},{7,31}} | collective-permute-start | bytes 746504 | tf_op jit(solution)/shard_map/ppermute | solution.py:178
  489.2 18.5 %collective-permute-start.31 = (bf16[144,3,288]{2,0,1:T(8,128)(2,1)S(1)}, bf16[144,3,288]{2,0,1:T(8,128)(2,1)S(1)}, u32[]{:S(2)}, u32[]{:S(2)}) collective-permute-start(bf16[144,3,288]{2,0,1:T(8,128)(2,1)S(1)} %get-tuple-element.92), channel_id=1, source_target_pairs={{16,0},{20,4},{24,8},{28,12},{17,1},{21,5},{25,9},{29,13},{18,2},{... | collective-permute-start | bytes 746504 | tf_op jit(solution)/shard_map/ppermute | solution.py:178
  490.6 17.2 %collective-permute-start.30 = (bf16[144,3,288]{2,0,1:T(8,128)(2,1)S(1)}, bf16[144,3,288]{2,0,1:T(8,128)(2,1)S(1)}, u32[]{:S(2)}, u32[]{:S(2)}) collective-permute-start(bf16[144,3,288]{2,0,1:T(8,128)(2,1)S(1)} %get-tuple-element.93), channel_id=1, source_target_pairs={{0,16},{4,20},{8,24},{12,28},{1,17},{5,21},{9,25},{13,29},{2,18},{... | collective-permute-start | bytes 746504 | tf_op jit(solution)/shard_map/ppermute | solution.py:178
  496.1 17.8 %collective-permute-start.29 = (bf16[144,3,288]{2,0,1:T(8,128)(2,1)S(1)}, bf16[144,3,288]{2,0,1:T(8,128)(2,1)S(1)}, u32[]{:S(2)}, u32[]{:S(2)}) collective-permute-start(bf16[144,3,288]{2,0,1:T(8,128)(2,1)S(1)} %get-tuple-element.94), channel_id=1, source_target_pairs={{8,0},{12,4},{16,8},{20,12},{24,16},{28,20},{9,1},{13,5},{17,9},{2... | collective-permute-start | bytes 746504 | tf_op jit(solution)/shard_map/ppermute | solution.py:178
  497.4 17.6 %collective-permute-start.17 = (bf16[288,1024]{1,0:T(8,128)(2,1)S(1)}, bf16[288,1024]{1,0:T(8,128)(2,1)S(1)}, u32[]{:S(2)}, u32[]{:S(2)}) collective-permute-start(bf16[288,1024]{1,0:T(8,128)(2,1)S(1)} %fusion.65), channel_id=1, source_target_pairs={{0,2},{1,3},{2,0},{3,1},{4,6},{5,7},{6,4},{7,5},{8,10},{9,11},{10,... | collective-permute-start | bytes 1769480 | tf_op jit(solution)/shard_map/ppermute | solution.py:173
  (100 other events, 1162.0 us)

commit v2 on v1

v2 whole, which is shorter than its diff:
```python
import functools
import math

import jax
import jax.numpy as jnp
from jax import lax
from jax.experimental import pallas as pl
from jax.experimental.pallas import tpu as pltpu
from jax.sharding import PartitionSpec as P

HD = 72
FACTOR = HD ** (-0.5)
LOG2E = math.log2(math.e)
NEG = -1e30
BQ = 256
BK = 256
F32 = jnp.float32
BF16 = jnp.bfloat16


def contract(a, b, dims):
    return lax.dot_general(a, b, (dims, ((), ())), preferred_element_type=F32)


def forward_kernel(bases, heads, last, bounds, span, query, mixed_in, top_in, total_in, *refs):
    segments = len(bases)
    keys = refs[:segments]
    values = refs[segments : 2 * segments]
    mixed_out, top_out, total_out, mixed = refs[2 * segments :]
    rows = query.shape[2]
    scale = FACTOR * LOG2E

    def query_block(i, _):
        own = pl.ds(pl.multiple_of(i * BQ, BQ), BQ)
        begin = span[0:1, own]
        end = span[1:2, own]
        for h in range(heads):
            mixed[h] = mixed_in[h, :, own]
        state = tuple(top_in[h, :, own] for h in range(heads)) + tuple(
            total_in[h, :, own] for h in range(heads)
        )
        for s, base in enumerate(bases):

            def key_block(j, state, s=s, base=base):
                k_at = pl.multiple_of(j * BK, BK)
                block = pl.ds(k_at, BK)
                place = lax.broadcasted_iota(jnp.int32, (BK, BQ), 0) + (k_at + base)
                allowed = (place >= begin) & (place < end)
                raws = [
                    contract(keys[s][h, :, block], query[h, :, own], ((0,), (0,)))
                    for h in range(heads)
                ]
                tops, totals, shrinks, lows = [], [], [], []
                for h in range(heads):
                    raw = jnp.where(allowed, raws[h] * scale, NEG)
                    top = jnp.maximum(state[h], jnp.max(raw, axis=0, keepdims=True))
                    probs = jnp.exp2(raw - top)
                    shrink = jnp.exp2(state[h] - top)
                    tops.append(top)
                    totals.append(state[heads + h] * shrink + jnp.sum(probs, axis=0, keepdims=True))
                    shrinks.append(shrink)
                    lows.append(probs.astype(BF16))
                for h in range(heads):
                    mixed[h] = mixed[h] * shrinks[h] + contract(
                        values[s][h, :, block], lows[h], ((1,), (0,))
                    )
                return tuple(tops) + tuple(totals)

            state = lax.fori_loop(bounds[s, 0, i], bounds[s, 1, i], key_block, state)
        for h in range(heads):
            top, total = state[h], state[heads + h]
            if last:
                mixed_out[h, :, own] = (mixed[h] / total).astype(BF16)
                top_out[h, :, own] = top + jnp.log2(total)
            else:
                mixed_out[h, :, own] = mixed[h]
                top_out[h, :, own] = top
            total_out[h, :, own] = total
        return 0

    lax.fori_loop(0, rows // BQ, query_block, 0)


def attend(bounds, span, query, carried, keys, values, bases, last):
    heads, hd, rows = query.shape
    vmem = pl.BlockSpec(memory_space=pltpu.VMEM)
    line = jax.ShapeDtypeStruct((heads, 1, rows), F32)
    return pl.pallas_call(
        functools.partial(forward_kernel, bases, heads, last),
        out_shape=(
            jax.ShapeDtypeStruct((heads, hd, rows), BF16 if last else F32),
            line,
            line,
        ),
        in_specs=[pl.BlockSpec(memory_space=pltpu.SMEM)] + [vmem] * (5 + 2 * len(bases)),
        out_specs=(vmem,) * 3,
        scratch_shapes=[pltpu.VMEM((heads, hd, BQ), F32)],
        compiler_params=pltpu.CompilerParams(vmem_limit_bytes=40 << 20),
        cost_estimate=pl.CostEstimate(
            flops=24 * heads * rows * rows * HD,
            bytes_accessed=24 << 20,
            transcendentals=heads * rows * rows,
        ),
    )(bounds, span, query, *carried, *keys, *values)


def tile_back(heads, allowed, keys, values, query, grad, logsum, delta):
    scale = FACTOR * LOG2E
    raws = [contract(keys[h], query[h], ((0,), (0,))) for h in range(heads)]
    grads = [contract(values[h], grad[h], ((0,), (0,))) for h in range(heads)]
    found = []
    for h in range(heads):
        raw = jnp.where(allowed, raws[h] * scale - logsum[h], NEG)
        probs = jnp.exp2(raw)
        found.append((probs.astype(BF16), (probs * (grads[h] - delta[h])).astype(BF16)))
    return found


def backward_kernel(bases, heads, bounds, span, query, grad, logsum, delta, *refs):
    segments = len(bases)
    keys = refs[:segments]
    values = refs[segments : 2 * segments]
    grad_query, grad_keys, grad_values, sum_query, sum_keys, sum_values = refs[2 * segments :]
    sum_query[...] = jnp.zeros_like(sum_query)
    for s, base in enumerate(bases):

        def key_block(j, _, s=s, base=base):
            k_at = pl.multiple_of(j * BK, BK)
            block = pl.ds(k_at, BK)
            place = lax.broadcasted_iota(jnp.int32, (BK, BQ), 0) + (k_at + base)
            if base == 0:
                sum_keys[...] = jnp.zeros_like(sum_keys)
                sum_values[...] = jnp.zeros_like(sum_values)

            def query_block(i, _):
                own = pl.ds(pl.multiple_of(i * BQ, BQ), BQ)
                allowed = (place >= span[0:1, own]) & (place < span[1:2, own])
                q = [query[h, :, own] for h in range(heads)]
                g = [grad[h, :, own] for h in range(heads)]
                k = [keys[s][h, :, block] for h in range(heads)]
                found = tile_back(
                    heads,
                    allowed,
                    k,
                    [values[s][h, :, block] for h in range(heads)],
                    q,
                    g,
                    [logsum[h, :, own] for h in range(heads)],
                    [delta[h, :, own] for h in range(heads)],
                )
                for h in range(heads):
                    probs, grad_raw = found[h]
                    if base == 0:
                        sum_values[h] += contract(g[h], probs, ((1,), (1,)))
                        sum_keys[h] += contract(q[h], grad_raw, ((1,), (1,)))
                    sum_query[h, :, own] += contract(k[h], grad_raw, ((1,), (0,)))
                return 0

            lax.fori_loop(bounds[s, 0, j], bounds[s, 1, j], query_block, 0)
            if base == 0:
                for h in range(heads):
                    grad_keys[h, :, block] = sum_keys[h]
                    grad_values[h, :, block] = sum_values[h]
            return 0

        lax.fori_loop(0, keys[s].shape[2] // BK, key_block, 0)
    grad_query[...] = (sum_query[...] * FACTOR).astype(BF16)


def attend_back(bounds, span, query, grad, logsum, delta, keys, values, bases):
    heads, hd, rows = query.shape
    vmem = pl.BlockSpec(memory_space=pltpu.VMEM)
    full = jax.ShapeDtypeStruct((heads, hd, rows), F32)
    return pl.pallas_call(
        functools.partial(backward_kernel, bases, heads),
        out_shape=(jax.ShapeDtypeStruct((heads, hd, rows), BF16), full, full),
        in_specs=[pl.BlockSpec(memory_space=pltpu.SMEM)] + [vmem] * (5 + 2 * len(bases)),
        out_specs=(vmem,) * 3,
        scratch_shapes=[
            pltpu.VMEM((heads, hd, rows), F32),
            pltpu.VMEM((heads, hd, BK), F32),
            pltpu.VMEM((heads, hd, BK), F32),
        ],
        compiler_params=pltpu.CompilerParams(vmem_limit_bytes=44 << 20),
        cost_estimate=pl.CostEstimate(
            flops=60 * heads * rows * rows * HD,
            bytes_accessed=30 << 20,
            transcendentals=heads * rows * rows,
        ),
    )(bounds, span, query, grad, logsum, delta, *keys, *values)


def others_kernel(segments, heads, bounds, keys, values, keys_in, values_in, *refs):
    spans, query, grad, logsum, delta = (refs[n * segments : (n + 1) * segments] for n in range(5))
    grad_keys, grad_values, sum_keys, sum_values = refs[5 * segments :]

    def key_block(j, _):
        k_at = pl.multiple_of(j * BK, BK)
        block = pl.ds(k_at, BK)
        place = lax.broadcasted_iota(jnp.int32, (BK, BQ), 0) + k_at
        for h in range(heads):
            sum_keys[h] = keys_in[h, :, block]
            sum_values[h] = values_in[h, :, block]
        for s in range(segments):

            def query_block(i, _, s=s):
                own = pl.ds(pl.multiple_of(i * BQ, BQ), BQ)
                allowed = (place >= spans[s][0:1, own]) & (place < spans[s][1:2, own])
                q = [query[s][h, :, own] for h in range(heads)]
                g = [grad[s][h, :, own] for h in range(heads)]
                found = tile_back(
                    heads,
                    allowed,
                    [keys[h, :, block] for h in range(heads)],
                    [values[h, :, block] for h in range(heads)],
                    q,
                    g,
                    [logsum[s][h, :, own] for h in range(heads)],
                    [delta[s][h, :, own] for h in range(heads)],
                )
                for h in range(heads):
                    probs, grad_raw = found[h]
                    sum_values[h] += contract(g[h], probs, ((1,), (1,)))
                    sum_keys[h] += contract(q[h], grad_raw, ((1,), (1,)))
                return 0

            lax.fori_loop(bounds[s, 0, j], bounds[s, 1, j], query_block, 0)
        for h in range(heads):
            grad_keys[h, :, block] = (sum_keys[h] * FACTOR).astype(BF16)
            grad_values[h, :, block] = sum_values[h].astype(BF16)
        return 0

    lax.fori_loop(0, keys.shape[2] // BK, key_block, 0)


def others_back(bounds, keys, values, keys_in, values_in, spans, query, grad, logsum, delta):
    heads, hd, rows = keys.shape
    segments = len(query)
    vmem = pl.BlockSpec(memory_space=pltpu.VMEM)
    shape = jax.ShapeDtypeStruct((heads, hd, rows), BF16)
    return pl.pallas_call(
        functools.partial(others_kernel, segments, heads),
        out_shape=(shape, shape),
        in_specs=[pl.BlockSpec(memory_space=pltpu.SMEM)] + [vmem] * (4 + 5 * segments),
        out_specs=(vmem, vmem),
        scratch_shapes=[pltpu.VMEM((heads, hd, BK), F32), pltpu.VMEM((heads, hd, BK), F32)],
        compiler_params=pltpu.CompilerParams(vmem_limit_bytes=40 << 20),
        cost_estimate=pl.CostEstimate(
            flops=30 * heads * rows * rows * HD,
            bytes_accessed=30 << 20,
            transcendentals=heads * rows * rows // 2,
        ),
    )(bounds, keys, values, keys_in, values_in, *spans, *query, *grad, *logsum, *delta)


def swap(value, axis, bit):
    return lax.ppermute(value, axis, [(i, i ^ bit) for i in range(lax.axis_size(axis))])


def shift(value, axis, distance):
    devices = range(lax.axis_size(axis))
    return lax.ppermute(value, axis, [(i, i + distance) for i in devices if i + distance in devices])


def bits_of(axis):
    size = lax.axis_size(axis)
    return [1 << b for b in range(size.bit_length() - 1)]


def bit_set(axis, bit):
    return (lax.axis_index(axis) & bit) != 0


def sum_all(value, axis):
    for bit in bits_of(axis):
        value = value + swap(value, axis, bit)
    return value


def after(anchor, *values):
    held = values if anchor is None else lax.optimization_barrier((anchor, *values))[1:]
    return held[0] if len(values) == 1 else held


def in_order(mine, other, upper, dim=0):
    return jnp.where(
        upper, jnp.stack([other, mine], axis=dim), jnp.stack([mine, other], axis=dim)
    )


def gather_tensor(value):
    pair = in_order(value, swap(value, "tensor", 2), bit_set("tensor", 2))
    quad = in_order(pair, swap(pair, "tensor", 1), bit_set("tensor", 1), dim=1)
    return quad.reshape((4 * value.shape[0],) + value.shape[1:])


def scatter_tensor(partial):
    n = partial.shape[0] // 4
    core = lax.axis_index("tensor") % 2
    across = lax.axis_index("tensor") // 2
    parts = partial.astype(BF16).reshape((2, 2, n) + partial.shape[1:])
    kept = lax.dynamic_index_in_dim(parts, core, 1, keepdims=False)
    sent = lax.dynamic_index_in_dim(parts, 1 - core, 1, keepdims=False)
    come = swap(sent, "tensor", 1)
    come = after((yield sent), come)
    half = kept.astype(F32) + come.astype(F32)
    half_low = half.astype(BF16)
    stay = lax.dynamic_index_in_dim(half, across, 0, keepdims=False)
    leave = lax.dynamic_index_in_dim(half_low, 1 - across, 0, keepdims=False)
    come = swap(leave, "tensor", 2)
    come = after((yield leave), come)
    return stay + come.astype(F32)


def scatter_data(partial):
    size = lax.axis_size("dp")
    index = lax.axis_index("dp")
    bits = bits_of("dp")
    count = len(bits)
    rest = (partial.shape[0] // size,) + partial.shape[1:]
    held = partial.astype(BF16).reshape((2,) * count + rest)
    left = list(reversed(bits))
    for bit in [1] + bits[:0:-1]:
        axis = left.index(bit)
        mine = (index // bit) % 2
        kept = lax.dynamic_index_in_dim(held, mine, axis, keepdims=False)
        sent = lax.dynamic_index_in_dim(held, 1 - mine, axis, keepdims=False).astype(BF16)
        come = swap(sent, "dp", bit)
        come = after((yield sent), come)
        held = kept.astype(F32) + come.astype(F32)
        left.remove(bit)
    return held


def finish(steps, anchor=None):
    try:
        while True:
            steps.send(anchor)
    except StopIteration as end:
        return end.value


def layer_norm(value):
    center = value - jnp.mean(value, axis=-1, keepdims=True)
    spread = jnp.mean(center * center, axis=-1, keepdims=True)
    return center * lax.rsqrt(spread + 1e-06)


def gelu_tanh(value):
    return jax.nn.gelu(value, approximate=True)


def onehot_sum(select, values, form):
    upper = values.astype(BF16)
    lower = (values - upper.astype(F32)).astype(BF16)
    first = jnp.einsum(form, select, upper, preferred_element_type=F32)
    return first + jnp.einsum(form, select, lower, preferred_element_type=F32)


def on_device(
    tokens,
    condition,
    latent_lengths,
    in_weight,
    in_bias,
    out_weight,
    out_bias,
    up_weight,
    up_bias,
    down_weight,
    down_bias,
    mod_weight,
    mod_bias,
    out_grad,
):
    rows, width = tokens.shape
    latents = condition.shape[0]
    local_width = in_weight.shape[2]
    heads = local_width // HD
    data_size = lax.axis_size("dp")
    data_index = lax.axis_index("dp")
    tensor_index = lax.axis_index("tensor")
    quarter = rows // 4
    row_start = tensor_index * quarter

    def mine(value):
        return lax.dynamic_slice_in_dim(value, row_start, quarter, 0)

    places = jnp.arange(latents, dtype=jnp.int32)
    earlier = places[None, :] < places[:, None]
    starts = jnp.sum(jnp.where(earlier, latent_lengths[None, :], 0), axis=1)
    ends = starts + latent_lengths
    first_row = data_index * rows
    own_places = first_row + jnp.arange(rows, dtype=jnp.int32)

    def span_of(at):
        inside = (at[:, None] >= starts[None, :]) & (at[:, None] < ends[None, :])
        begin = jnp.sum(jnp.where(inside, starts[None, :] - first_row, 0), axis=1)
        end = jnp.sum(jnp.where(inside, ends[None, :] - first_row, 0), axis=1)
        return begin, end, inside

    bases = (-rows, 0, rows)
    windows = [span_of(own_places + base) for base in bases]
    spans = [jnp.stack(window[:2]) for window in windows]
    selects = [window[2].astype(BF16) for window in windows]
    begin, end = windows[1][:2]
    span, select = spans[1], selects[1]
    select_mine = mine(select)
    forward_bounds, backward_bounds, other_bounds = [], [], []
    for base in bases:
        low = jnp.clip(begin[::BQ] - base, 0, rows) // BK
        high = (jnp.clip(end[BQ - 1 :: BQ] - base, 0, rows) + BK - 1) // BK
        forward_bounds.append(jnp.stack([low, high]))
        key_at = first_row + base + jnp.arange(rows // BK, dtype=jnp.int32) * BK
        low = jnp.clip(span_of(key_at)[0], 0, rows) // BQ
        high = (jnp.clip(span_of(key_at + BK - 1)[1], 0, rows) + BQ - 1) // BQ
        valid = (key_at >= 0) & (key_at < rows * data_size)
        backward_bounds.append(jnp.where(valid[None, :], jnp.stack([low, high]), 0))
        low = jnp.clip(begin[::BK] - base, 0, rows) // BQ
        high = (jnp.clip(end[BK - 1 :: BK] - base, 0, rows) + BQ - 1) // BQ
        other_bounds.append(jnp.stack([low, high]))
    backward_bounds = jnp.stack(backward_bounds)
    other_bounds = jnp.stack([other_bounds[0], other_bounds[2]])

    tokens_mine = mine(tokens)
    behind_tokens = gather_tensor(shift(tokens_mine, "dp", 1))
    ahead_tokens = gather_tensor(shift(tokens_mine, "dp", -1))

    cond_full = condition.astype(F32)
    silu_cond = jax.nn.silu(cond_full).astype(BF16)
    mod_local = (
        jnp.dot(silu_cond, mod_weight, preferred_element_type=F32) + mod_bias.astype(F32)
    ).astype(BF16)
    modulation = gather_tensor(mod_local[None])
    modulation = modulation.transpose(1, 0, 2).reshape(latents, 6 * width)

    def spread(chosen, first, count):
        return jnp.dot(
            chosen,
            modulation[:, first * width : (first + count) * width],
            preferred_element_type=BF16,
        )

    others = spread(select_mine, 2, 4).astype(F32)
    gate_a, shift_m, scale_m, gate_m = (others[:, i * width : (i + 1) * width] for i in range(4))
    gate_m_all = spread(select, 5, 1).astype(F32)

    bias_full = in_bias.astype(F32)
    proj_bias = jnp.stack([bias_full[0], jnp.zeros_like(bias_full[0]), bias_full[1]])

    def entry_of(rows_of, chosen):
        shift_scale = spread(chosen, 0, 2)
        scale = shift_scale[:, width:].astype(F32)
        value = rows_of.astype(F32)
        center = value - jnp.mean(value, axis=-1, keepdims=True)
        inverse = lax.rsqrt(jnp.mean(center * center, axis=-1, keepdims=True) + 1e-06)
        normed = center * inverse
        entry = (normed * (1.0 + scale) + shift_scale[:, :width].astype(F32)).astype(BF16)
        return entry, normed, inverse

    def project(entry):
        found = jnp.einsum("dcf,td->cft", in_weight, entry, preferred_element_type=F32)
        found = (found + proj_bias[:, :, None]).astype(BF16)
        return found.reshape(3, heads, HD, rows)

    entry, normed, inverse = entry_of(tokens, select)
    normed_turned, inverse = normed.T, inverse.T
    own = project(entry)
    sides = [
        project(entry_of(behind_tokens, selects[0])[0]),
        project(entry_of(ahead_tokens, selects[2])[0]),
    ]
    query = own[0]
    line = jnp.zeros((heads, 1, rows), F32)
    carried = attend(
        jnp.stack([forward_bounds[1]]),
        span,
        query,
        (jnp.zeros((heads, HD, rows), F32), line + NEG, line),
        [own[1]],
        [own[2]],
        (0,),
        False,
    )
    attended, logsum, _ = attend(
        jnp.stack([forward_bounds[0], forward_bounds[2]]),
        span,
        query,
        carried,
        [side[1] for side in sides],
        [side[2] for side in sides],
        (-rows, rows),
        True,
    )
    attended_flat = attended.reshape(local_width, rows)
    attn_part = lax.dot_general(
        attended_flat, out_weight, (((0,), (1,)), ((), ())), preferred_element_type=F32
    )
    attn_steps = scatter_tensor(attn_part)
    next(attn_steps)
    branch = finish(attn_steps) + out_bias.astype(F32)

    middle = tokens_mine.astype(F32) + gate_a * branch
    normed_m, norm_back_m = jax.vjp(layer_norm, middle)
    entry_m = gather_tensor((normed_m * (1.0 + scale_m) + shift_m).astype(BF16))
    hidden_pre = jnp.dot(entry_m, up_weight, preferred_element_type=F32) + up_bias.astype(F32)
    hidden_full, gelu_back = jax.vjp(gelu_tanh, hidden_pre)
    hidden = hidden_full.astype(BF16)
    grad_out = out_grad.astype(F32)
    grad_branch_m = (gate_m_all * grad_out).astype(BF16)
    grad_hidden = jnp.einsum("td,df->tf", grad_branch_m, down_weight, preferred_element_type=F32)
    grad_pre = gelu_back(grad_hidden)[0].astype(BF16)
    grad_down_w = jnp.einsum("td,tf->df", grad_branch_m, hidden, preferred_element_type=F32)
    down_steps = scatter_data(grad_down_w)
    down_sent = next(down_steps)
    grad_pre = after(down_sent, grad_pre)
    entry_part = jnp.einsum("tf,df->td", grad_pre, up_weight, preferred_element_type=F32)
    entry_steps = scatter_tensor(entry_part)
    grad_pre = after(next(entry_steps), grad_pre)
    grad_out_mine = mine(out_grad).astype(F32)
    grad_up_w = jnp.einsum("td,tf->df", entry_m, grad_pre, preferred_element_type=F32)
    up_steps = scatter_data(grad_up_w)
    up_sent = next(up_steps)
    grad_entry_m = finish(entry_steps, up_sent)
    grad_down_b = jnp.sum(grad_branch_m.astype(F32), axis=0)
    grad_up_b = jnp.sum(grad_pre.astype(F32), axis=0)
    grad_middle = grad_out_mine + norm_back_m(grad_entry_m * (1.0 + scale_m))[0]
    grad_gate_a = grad_middle * branch
    grad_branch_mine = (gate_a * grad_middle).astype(BF16)
    grad_out_b = jnp.sum(grad_branch_mine.astype(F32), axis=0)
    grad_branch = gather_tensor(grad_branch_mine)
    grad_attended = lax.dot_general(
        out_weight, grad_branch, (((0,), (1,)), ((), ())), preferred_element_type=F32
    ).astype(BF16)

    mlp_part = jnp.einsum(
        "tf,df->td",
        after(grad_branch_mine, hidden),
        down_weight,
        preferred_element_type=F32,
    )
    mlp_steps = scatter_tensor(mlp_part)
    next(mlp_steps)

    grad_heads = grad_attended.reshape(heads, HD, rows)
    delta = jnp.sum(grad_heads.astype(F32) * attended.astype(F32), axis=1, keepdims=True)
    stats = jnp.stack([logsum, delta])
    side_grads = [shift(grad_heads, "dp", 1), shift(grad_heads, "dp", -1)]
    side_stats = [shift(stats, "dp", 1), shift(stats, "dp", -1)]
    grad_query, part_keys, part_values = attend_back(
        backward_bounds,
        span,
        query,
        grad_heads,
        logsum,
        delta,
        [sides[0][1], own[1], sides[1][1]],
        [sides[0][2], own[2], sides[1][2]],
        bases,
    )
    mlp_steps.send(grad_heads)
    down_steps.send(grad_heads)
    up_steps.send(grad_query)
    branch_m = finish(mlp_steps, grad_query) + down_bias.astype(F32)
    output = (middle + gate_m * branch_m).astype(BF16)
    grad_gate_m = grad_out_mine * branch_m
    grad_out_w = lax.dot_general(
        grad_branch, attended_flat, (((0,), (1,)), ((), ())), preferred_element_type=F32
    )
    grad_keys, grad_values = others_back(
        other_bounds,
        own[1],
        own[2],
        part_keys,
        part_values,
        [spans[0], spans[2]],
        [side[0] for side in sides],
        side_grads,
        [side[0] for side in side_stats],
        [side[1] for side in side_stats],
    )
    grad_proj = [x.reshape(local_width, rows) for x in (grad_query, grad_keys, grad_values)]
    grad_q_w, grad_k_w, grad_v_w = (
        lax.dot_general(entry, x, (((0,), (1,)), ((), ())), preferred_element_type=F32)
        for x in grad_proj
    )
    early_steps = scatter_data(jnp.concatenate([grad_out_w, grad_q_w], axis=1))
    next(early_steps)
    late_steps = scatter_data(jnp.concatenate([grad_k_w, grad_v_w], axis=1))
    late_sent = next(late_steps)
    early_steps.send(late_sent)
    grad_proj = after(late_sent, *grad_proj)
    grad_in_b = jnp.stack([jnp.sum(grad_proj[c].astype(F32), axis=1) for c in (0, 2)])
    grad_entry = lax.dot_general(
        in_weight.reshape(width, 3 * local_width),
        jnp.concatenate(grad_proj, axis=0),
        (((1,), (0,)), ((), ())),
        preferred_element_type=F32,
    )
    scale_turned = lax.dot_general(
        modulation[:, width : 2 * width],
        select,
        (((0,), (1,)), ((), ())),
        preferred_element_type=BF16,
    ).astype(F32)
    scaled = grad_entry * (1.0 + scale_turned)
    input_part = (
        scaled
        - jnp.mean(scaled, axis=0, keepdims=True)
        - normed_turned * jnp.mean(scaled * normed_turned, axis=0, keepdims=True)
    ) * inverse

    split_terms = jnp.concatenate([grad_entry, grad_entry * normed_turned], axis=0)
    kept_terms = jnp.concatenate(
        [grad_gate_a, grad_entry_m, grad_entry_m * normed_m, grad_gate_m], axis=1
    )
    per_latent = jnp.concatenate(
        [onehot_sum(select, split_terms, "tl,mt->lm"), onehot_sum(select_mine, kept_terms, "tl,tm->lm")],
        axis=1,
    )
    columns_here = mod_weight.shape[1]
    arranged = per_latent.reshape(latents, 4, columns_here).transpose(1, 0, 2)
    arranged = arranged.reshape(4, latents * columns_here)

    def for_device(flip):
        chosen = lax.dynamic_index_in_dim(arranged, tensor_index ^ flip, 0, keepdims=False)
        return jnp.concatenate([chosen, grad_out_b])

    given = [for_device(flip) for flip in range(4)]
    come = [swap(given[flip], "tensor", flip) for flip in (1, 2, 3)]
    placed = lax.dynamic_update_slice_in_dim(
        jnp.zeros((width, rows), F32), grad_middle.T, row_start, 1
    )
    tokens_steps = scatter_tensor(input_part + placed)
    tokens_sent = next(tokens_steps)
    come = after(tokens_sent, *come)
    small = (given[0] + come[0]) + (come[1] + come[2])
    small = jnp.concatenate([small, grad_in_b.reshape(-1), grad_up_b, grad_down_b])
    tokens_sent = tokens_steps.send(small)
    for place, bit in enumerate(bits_of("dp")):
        come = swap(small, "dp", bit)
        if place == 0:
            come = after(tokens_sent, come)
        small = small + come
        if place == 0:
            up_steps.send(small)
        if place == 1:
            late_sent = late_steps.send(small)
            small = after(late_sent, small)
    cuts, at = [], 0
    for size in (latents * columns_here, width, 2 * local_width, grad_up_b.shape[0]):
        at += size
        cuts.append(at)
    grad_mod, sum_out_b, sum_in_b, sum_up_b, sum_down_b = jnp.split(small, cuts)
    grad_mod = grad_mod.reshape(latents, columns_here).astype(BF16)
    own_width = width // data_size
    own_silu = lax.dynamic_slice_in_dim(silu_cond, data_index * own_width, own_width, 1)
    grad_mod_w = jnp.einsum("ld,lm->dm", own_silu, grad_mod, preferred_element_type=F32)
    grad_mod_b = jnp.sum(grad_mod.astype(F32), axis=0)
    own_count = latents // data_size
    own_grad_mod = lax.dynamic_slice_in_dim(grad_mod, data_index * own_count, own_count, 0)
    own_cond = lax.dynamic_slice_in_dim(cond_full, data_index * own_count, own_count, 0)
    silu_grad = jnp.einsum("lm,dm->ld", own_grad_mod, mod_weight, preferred_element_type=F32)
    cond_part = jax.vjp(jax.nn.silu, own_cond)[1](silu_grad)[0]
    cond_parts = cond_part.reshape(own_count, 4, width // 4).transpose(1, 0, 2)
    grad_cond = lax.dynamic_index_in_dim(cond_parts, tensor_index, 0, keepdims=False)
    for bit in (1, 2, 3):
        grad_cond = grad_cond + swap(
            lax.dynamic_index_in_dim(cond_parts, tensor_index ^ bit, 0, keepdims=False),
            "tensor",
            bit,
        )

    grad_tokens = finish(tokens_steps, grad_mod_w).T
    sum_down_w = finish(down_steps, grad_keys)
    sum_up_w = finish(up_steps, grad_mod_w)
    early = finish(early_steps, grad_mod_w)
    late = finish(late_steps)
    sum_out_w = early[:, :local_width]
    sum_in_w = jnp.stack(
        [early[:, local_width:], late[:, :local_width], late[:, local_width:]], axis=1
    )
    return (
        output,
        grad_tokens,
        grad_cond,
        sum_in_w,
        sum_in_b.reshape(2, local_width),
        sum_out_w,
        sum_out_b,
        sum_up_w,
        sum_up_b,
        sum_down_w,
        sum_down_b,
        grad_mod_w,
        grad_mod_b,
    )


def solution(mesh):
    placed = (
        P("dp", None),
        P(),
        P(),
        P(None, None, "tensor"),
        P(None, "tensor"),
        P(None, "tensor"),
        P(),
        P(None, "tensor"),
        P("tensor"),
        P(None, "tensor"),
        P(),
        P(None, "tensor"),
        P("tensor"),
        P("dp", None),
    )
    return jax.shard_map(
        on_device,
        mesh=mesh,
        in_specs=placed,
        out_specs=(
            P(("dp", "tensor"), None),
            P("dp", "tensor"),
            P("dp", "tensor"),
            P("dp", None, "tensor"),
            P(None, "tensor"),
            P("dp", "tensor"),
            P(),
            P("dp", "tensor"),
            P("tensor"),
            P("dp", "tensor"),
            P(),
            P("dp", "tensor"),
            P("tensor"),
        ),
        check_vma=False,
    )
```

time: 524 us -> 428 us (0.82)
  starting transfers between devices: 151 us -> 76.1 us
  waiting for transfers between devices: 155 us -> 107 us
  other arithmetic: 61.1 us -> 81.4 us
  local copies, waits for them, and re-layouts: 35 us -> 53.1 us
  Pallas kernels: 46.9 us -> 38.1 us
    ppermute x28 -> x6, waiting for transfers between devices: 90.6 us -> 0.02 us  [shift(): lax.ppermute(value, axis, [(i, i + distance) for i in devices if i + dist...]
    ppermute x28 -> x6, starting transfers between devices: 103 us -> 24.3 us  [shift(): lax.ppermute(value, axis, [(i, i + distance) for i in devices if i + dist...]
    ppermute x32 -> x39, waiting for transfers between devices: 64.6 us -> 107 us  [swap(): lax.ppermute(value, axis, [(i, i ^ bit) for i in range(lax.axis_size(axis...]
    select_n x9 -> x13, other arithmetic: 1.7 us -> 11.1 us  [in_order(): jnp.where(upper, jnp.stack([other, mine], axis=dim), jnp.stack([mine, oth...]
    reduce_sum x0 -> x8, other arithmetic: none -> 9.36 us  [the longest x3 3.57 us: entry_of(): center = value - jnp.mean(value, axis=-1, keepdims=True)]
    reduce_sum x4 -> x2, other arithmetic: 10.9 us -> 2.1 us  [layer_norm(): center = value - jnp.mean(value, axis=-1, keepdims=True)]
    dot_general x0 -> x2, local copies, waits for them, and re-layouts: none -> 8.79 us  [the longest x1 4.48 us: on_device(): lax.dot_general(entry, x, (((0,), (1,)), ((), ())), preferred_element_typ...]
    add x17 -> x23, other arithmetic: 12 us -> 20.4 us  [the longest x12 15.8 us: scatter_data(): held = kept.astype(F32) + come.astype(F32)]
  transfers between devices with their start and end apart: 60 -> 45, of which waited for: 18 -> 15; matrix products, arithmetic and copies ran while one was open for 18% -> 32% of each run, Pallas kernels for 5% -> 8%
where the time goes in v2:
time: 428 us; the launch traced here: 423 us
  waiting for transfers between devices  107 us (25%)
  other arithmetic  81.4 us (19%)
  starting transfers between devices  76.1 us (18%)
  matrix products  64.8 us (15%)
  local copies, waits for them, and re-layouts  53.1 us (12%)
  Pallas kernels  38.1 us (9%)
    ppermute x39, waiting for transfers between devices, swap(): lax.ppermute(value, axis, [(i, i ^ bit) for i in range(lax.axis_size(axis...  107 us
    ppermute x39, starting transfers between devices, swap(): lax.ppermute(value, axis, [(i, i ^ bit) for i in range(lax.axis_size(axis...  51.8 us
    ppermute x6, starting transfers between devices, shift(): lax.ppermute(value, axis, [(i, i + distance) for i in devices if i + dist...  24.3 us
    unnamed x217, local copies, waits for them, and re-layouts  16.8 us
    pallas_call x1, Pallas kernels, attend_back(): pl.pallas_call(functools.partial(backward_kernel, bases, heads), out_shap...  16.7 us
    add x12, other arithmetic, scatter_data(): held = kept.astype(F32) + come.astype(F32)  15.8 us
    pallas_call x2, Pallas kernels, attend(): pl.pallas_call(functools.partial(forward_kernel, bases, heads, last), out...  14.6 us
    select_n x13, other arithmetic, in_order(): jnp.where(upper, jnp.stack([other, mine], axis=dim), jnp.stack([mine, oth...  11.1 us
  transfers between devices with their start and end apart: 45, of which 15 were waited for; matrix products, arithmetic and copies ran while one was open for 32% of the time, Pallas kernels for 8%

profile of v2, /device:TPU:0, one launch (start us, length us, event | category | flops | bytes accessed | tf_op | source)
XLA Modules:
  0.0 423.2 jit_solution(10291664035280062191)
XLA Ops:
  2.7 5.7 %collective-permute-start.2 = (bf16[256,1152]{1,0:T(8,128)(2,1)}, bf16[256,1152]{1,0:T(8,128)(2,1)}, u32[]{:S(2)}, u32[]{:S(2)}) collective-permute-start(bf16[256,1152]{1,0:T(8,128)(2,1)} %constant_dynamic-slice_fusion.12), channel_id=1, source_target_pairs={{0,4},{4,8},{8,12},{12,16},{16,20},{20,24},{24,28},{1,5},{5,9},{9,... | collective-permute-start | bytes 1769480 | tf_op jit(solution)/shard_map/ppermute | solution.py:262
  10.4 3.3 fusion.46
  25.0 2.5 fusion.47
  28.4 9.1 %shard_map.237 = (f32[4,72,1024]{2,1,0:T(8,128)S(1)}, f32[4,1,1024]{2,1,0:T(1,128)S(1)}, f32[4,1,1024]{2,1,0:T(1,128)S(1)}) custom-call(s32[1,2,4]{2,1,0:T(2,128)S(1)} %add_bitcast_fusion.2.bounds, s32[2,1024]{1,0:T(2,128)S(1)} %pad_add_fusion.span, bf16[4,72,1024]{2,1,0:T(8,128)(2,1)S(1)} %bitcast.441, f32[4,72,1024]{2,1,0:T(8,128)S(1)} %broadcast_in_dim.200.mixed_in, ...), custom_call_target="tpu_custom_call" | custom-call | flops 7247757312 | bytes 25165824 | tf_op jit(solution)/shard_map/pallas_call | solution.py:88
  39.1 5.0 %collective-permute-done.6 = bf16[256,1152]{1,0:T(8,128)(2,1)S(1)} collective-permute-done((bf16[256,1152]{1,0:T(8,128)(2,1)}, bf16[256,1152]{1,0:T(8,128)(2,1)S(1)}, u32[]{:S(2)}, u32[]{:S(2)}) %collective-permute-start.6) | collective-permute-done | bytes 589856 | tf_op jit(solution)/shard_map/ppermute | solution.py:257
  48.7 7.3 %collective-permute-done.3 = bf16[256,1152]{1,0:T(8,128)(2,1)S(1)} collective-permute-done((bf16[256,1152]{1,0:T(8,128)(2,1)}, bf16[256,1152]{1,0:T(8,128)(2,1)S(1)}, u32[]{:S(2)}, u32[]{:S(2)}) %collective-permute-start.3) | collective-permute-done | bytes 589856 | tf_op jit(solution)/shard_map/ppermute | solution.py:257
  67.4 2.5 fusion.48
  72.7 2.5 fusion.49
  76.2 5.5 %shard_map.238 = (bf16[4,72,1024]{2,1,0:T(8,128)(2,1)S(1)}, f32[4,1,1024]{2,1,0:T(1,128)S(1)}, f32[4,1,1024]{2,1,0:T(1,128)}) custom-call(s32[2,2,4]{2,1,0:T(2,128)S(1)} %pad_add_fusion.4.bounds, s32[2,1024]{1,0:T(2,128)S(1)} %pad_add_fusion.span, bf16[4,72,1024]{2,1,0:T(8,128)(2,1)S(1)} %bitcast.442, f32[4,72,1024]{2,1,0:T(8,128)S(1)} %get-tuple-element.50.mixed_in, ...), custom_call_target="tpu_custom_call" | custom-call | flops 7247757312 | bytes 25165824 | tf_op jit(solution)/shard_map/pallas_call | solution.py:88
  95.3 13.9 %collective-permute-done.9 = bf16[256,1152]{1,0:T(8,128)(2,1)} collective-permute-done((bf16[256,1152]{1,0:T(8,128)(2,1)}, bf16[256,1152]{1,0:T(8,128)(2,1)}, u32[]{:S(2)}, u32[]{:S(2)}) %collective-permute-start.9) | collective-permute-done | bytes 589856 | tf_op jit(solution)/shard_map/ppermute | solution.py:257
  118.7 9.3 %collective-permute-done.10 = bf16[256,1152]{1,0:T(8,128)(2,1)} collective-permute-done((bf16[256,1152]{1,0:T(8,128)(2,1)}, bf16[256,1152]{1,0:T(8,128)(2,1)}, u32[]{:S(2)}, u32[]{:S(2)}) %collective-permute-start.10) | collective-permute-done | bytes 589856 | tf_op jit(solution)/shard_map/ppermute | solution.py:257
  131.6 3.5 fusion.158
  137.6 5.8 %fusion.22 = (bf16[1024,1152]{1,0:T(8,128)(2,1)S(1)}, bf16[1024,1152]{1,0:T(8,128)(2,1)S(1)}) fusion(f32[1024,1152]{1,0:T(8,128)S(1)} %fusion.158, f32[1152]{0:T(1024)S(1)} %copy-done.89, bf16[1024,1152]{1,0:T(8,128)(2,1)S(1)} %bitcast.503, bf16[1152,1152]{1,0:T(8,128)(2,1)S(1)} %copy-done), kind=kOutput, calls=%fused_computation.31 | convolution fusion | flops 2745040896 | bytes 14455296 | tf_op jit(solution)/shard_map/dot_general | solution.py:506
  143.4 3.3 convolution_convert_fusion.1
  149.5 3.8 convolution_convert_fusion.5
  154.0 3.3 convolution_convert_fusion
  161.2 14.9 %collective-permute-done.13 = bf16[256,1152]{1,0:T(8,128)(2,1)S(1)} collective-permute-done((bf16[256,1152]{1,0:T(8,128)(2,1)S(1)}, bf16[256,1152]{1,0:T(8,128)(2,1)S(1)}, u32[]{:S(2)}, u32[]{:S(2)}) %collective-permute-start.13) | collective-permute-done | bytes 589856 | tf_op jit(solution)/shard_map/ppermute | solution.py:257
  180.3 2.5 convert_reduce_fusion.5
  184.0 4.5 %copy.85 = bf16[1152,1024]{1,0:T(8,128)(2,1)} copy(bf16[1152,1024]{0,1:T(8,128)(2,1)} %bitcast.481) | data formatting | bytes 4718592 | tf_op jit(solution)/shard_map/dot_general | solution.py:584
  188.5 6.9 %collective-permute-start.42 = (bf16[2,2,144,1152]{3,2,1,0:T(8,128)(2,1)}, bf16[2,2,144,1152]{3,2,1,0:T(8,128)(2,1)S(1)}, u32[]{:S(2)}, u32[]{:S(2)}) collective-permute-start(bf16[2,2,144,1152]{3,2,1,0:T(8,128)(2,1)} %dynamic-slice_bitcast_fusion.1), channel_id=1, source_target_pairs={{0,4},{4,0},{8,12},{12,8},{16,20},{20,16},{24,28},{28,24},{1,5},{5... | collective-permute-start | bytes 3981320 | tf_op jit(solution)/shard_map/ppermute | solution.py:257
  195.4 2.6 convert_reduce_fusion.2
  198.4 5.2 %convolution_convert_fusion.4 = bf16[1024,1152]{1,0:T(8,128)(2,1)S(1)} fusion(bf16[1024,1152]{1,0:T(8,128)(2,1)} %copy-done.102, bf16[1152,1152]{1,0:T(8,128)(2,1)S(1)} %copy-done.97), kind=kOutput, calls=%fused_computation.55 | convolution fusion | flops 2719088640 | bytes 7372800 | tf_op jit(solution)/shard_map/tf,df->td/dot_general | solution.py:536
  209.1 8.8 %collective-permute-start.20 = (f32[2,4,1,1024]{3,2,1,0:T(1,128)S(1)}, f32[2,4,1,1024]{3,2,1,0:T(1,128)S(1)}, u32[]{:S(2)}, u32[]{:S(2)}) collective-permute-start(f32[2,4,1,1024]{3,2,1,0:T(1,128)S(1)} %pad_maximum_fusion.8), channel_id=1, source_target_pairs={{0,4},{4,8},{8,12},{12,16},{16,20},{20,24},{24,28},{1,5},{5,9},{9,... | collective-permute-start | bytes 98312 | tf_op jit(solution)/shard_map/ppermute | solution.py:262
  217.9 8.0 %collective-permute-done.42 = bf16[2,2,144,1152]{3,2,1,0:T(8,128)(2,1)S(1)} collective-permute-done((bf16[2,2,144,1152]{3,2,1,0:T(8,128)(2,1)}, bf16[2,2,144,1152]{3,2,1,0:T(8,128)(2,1)S(1)}, u32[]{:S(2)}, u32[]{:S(2)}) %collective-permute-start.42) | collective-permute-done | bytes 1327136 | tf_op jit(solution)/shard_map/ppermute | solution.py:257
  227.3 5.7 %collective-permute-start.18 = (bf16[4,72,1024]{2,1,0:T(8,128)(2,1)S(1)}, bf16[4,72,1024]{2,1,0:T(8,128)(2,1)}, u32[]{:S(2)}, u32[]{:S(2)}) collective-permute-start(bf16[4,72,1024]{2,1,0:T(8,128)(2,1)S(1)} %bitcast.461), channel_id=1, source_target_pairs={{0,4},{4,8},{8,12},{12,16},{16,20},{20,24},{24,28},{1,5},{5,9},{9,... | collective-permute-start | bytes 1769480 | tf_op jit(solution)/shard_map/ppermute | solution.py:262
  235.5 16.7 %shard_map.239 = (bf16[4,72,1024]{2,1,0:T(8,128)(2,1)S(1)}, f32[4,72,1024]{2,1,0:T(8,128)S(1)}, f32[4,72,1024]{2,1,0:T(8,128)S(1)}) custom-call(s32[3,2,4]{2,1,0:T(2,128)S(1)} %pad_add_fusion.3.bounds, s32[2,1024]{1,0:T(2,128)S(1)} %pad_add_fusion.span, bf16[4,72,1024]{2,1,0:T(8,128)(2,1)S(1)} %bitcast.443, bf16[4,72,1024]{2,1,0:T(8,128)(2,1)S(1)} %bitcast.462, ...), custom_call_target="tpu_custom_call" | custom-call | flops 18119393280 | bytes 31457280 | tf_op jit(solution)/shard_map/pallas_call | solution.py:174
  252.3 14.7 %collective-permute-done.39 = bf16[2,2,144,1152]{3,2,1,0:T(8,128)(2,1)S(1)} collective-permute-done((bf16[2,2,144,1152]{3,2,1,0:T(8,128)(2,1)}, bf16[2,2,144,1152]{3,2,1,0:T(8,128)(2,1)S(1)}, u32[]{:S(2)}, u32[]{:S(2)}) %collective-permute-start.39) | collective-permute-done | bytes 1327136 | tf_op jit(solution)/shard_map/ppermute | solution.py:257
  273.0 4.3 %copy.89 = bf16[1152,1024]{1,0:T(8,128)(2,1)} copy(bf16[1152,1024]{0,1:T(8,128)(2,1)} %bitcast.480) | data formatting | bytes 4718592 | tf_op jit(solution)/shard_map/dot_general | solution.py:567
  279.6 3.2 fusion.64
  284.3 2.6 fusion.87
  288.0 6.7 %collective-permute-start.43 = (bf16[2,144,1152]{2,1,0:T(8,128)(2,1)}, bf16[2,144,1152]{2,1,0:T(8,128)(2,1)}, u32[]{:S(2)}, u32[]{:S(2)}) collective-permute-start(bf16[2,144,1152]{2,1,0:T(8,128)(2,1)} %fusion.88), channel_id=1, source_target_pairs={{0,16},{4,20},{8,24},{12,28},{16,0},{20,4},{24,8},{28,12},{1,17},{... | collective-permute-start | bytes 1990664 | tf_op jit(solution)/shard_map/ppermute | solution.py:257
  295.1 2.8 convert_multiply_fusion
  300.3 6.8 %shard_map.240 = (bf16[4,72,1024]{2,1,0:T(8,128)(2,1)S(1)}, bf16[4,72,1024]{2,1,0:T(8,128)(2,1)S(1)}) custom-call(s32[2,2,4]{2,1,0:T(2,128)S(1)} %pad_add_fusion.4.bounds, bf16[4,72,1024]{2,1,0:T(8,128)(2,1)S(1)} %bitcast.440, bf16[4,72,1024]{2,1,0:T(8,128)(2,1)S(1)} %bitcast.437, f32[4,72,1024]{2,1,0:T(8,128)S(1)} %copy-done.19, ...), custom_call_target="tpu_custom_call" | custom-call | flops 9059696640 | bytes 31457280 | tf_op jit(solution)/shard_map/pallas_call | solution.py:241
  311.1 6.5 %collective-permute-start.28 = (bf16[2,2,144,576]{3,2,1,0:T(8,128)(2,1)}, bf16[2,2,144,576]{3,2,1,0:T(8,128)(2,1)}, u32[]{:S(2)}, u32[]{:S(2)}) collective-permute-start(bf16[2,2,144,576]{3,2,1,0:T(8,128)(2,1)} %fusion.85), channel_id=1, source_target_pairs={{0,4},{4,0},{8,12},{12,8},{16,20},{20,16},{24,28},{28,24},{1,5},{5... | collective-permute-start | bytes 1990664 | tf_op jit(solution)/shard_map/ppermute | solution.py:257
  318.0 2.9 convolution_bitcast_fusion
  330.3 4.1 convert_element_type.439
  334.4 3.0 copy.87
  346.3 3.4 collective-permute-start.44
  349.9 10.4 %collective-permute-done.44 = bf16[144,1152]{1,0:T(8,128)(2,1)} collective-permute-done((bf16[144,1152]{1,0:T(8,128)(2,1)S(1)}, bf16[144,1152]{1,0:T(8,128)(2,1)}, u32[]{:S(2)}, u32[]{:S(2)}) %collective-permute-start.44) | collective-permute-done | bytes 331808 | tf_op jit(solution)/shard_map/ppermute | solution.py:257
  369.5 2.7 collective-permute-done.27
  374.5 5.1 %collective-permute-start.29 = (f32[31680]{0:T(1024)S(1)}, f32[31680]{0:T(1024)S(1)}, u32[]{:S(2)}, u32[]{:S(2)}) collective-permute-start(f32[31680]{0:T(1024)S(1)} %add.755), channel_id=1, source_target_pairs={{0,16},{4,20},{8,24},{12,28},{16,0},{20,4},{24,8},{28,12},{1,17},{... | collective-permute-start | bytes 380168 | tf_op jit(solution)/shard_map/ppermute | solution.py:257
  382.1 2.5 collective-permute-done.29
  385.5 2.9 fusion.117
  397.5 2.7 collective-permute-start.36
  402.8 7.2 %collective-permute-done.36 = bf16[144,576]{1,0:T(8,128)(2,1)S(1)} collective-permute-done((bf16[144,576]{1,0:T(8,128)(2,1)S(1)}, bf16[144,576]{1,0:T(8,128)(2,1)S(1)}, u32[]{:S(2)}, u32[]{:S(2)}) %collective-permute-start.36) | collective-permute-done | bytes 165920 | tf_op jit(solution)/shard_map/ppermute | solution.py:257
  411.8 3.8 collective-permute-done.37
  415.8 2.4 fusion.73
  418.2 3.6 collective-permute-done.38
  (467 shorter events, 153.9 us)
Async XLA Ops:
  0.6 136.7 %copy-start = (bf16[1152,1152]{1,0:T(8,128)(2,1)S(1)}, bf16[1152,1152]{1,0:T(8,128)(2,1)}, u32[]{:S(2)}) copy-start(bf16[1152,1152]{1,0:T(8,128)(2,1)} %param.21) | copy-start | bytes 7962628
  2.7 34.8 %collective-permute-start.2 = (bf16[256,1152]{1,0:T(8,128)(2,1)}, bf16[256,1152]{1,0:T(8,128)(2,1)}, u32[]{:S(2)}, u32[]{:S(2)}) collective-permute-start(bf16[256,1152]{1,0:T(8,128)(2,1)} %constant_dynamic-slice_fusion.12), channel_id=1, source_target_pairs={{0,4},{4,8},{8,12},{12,16},{16,20},{20,24},{24,28},{1,5},{5,9},{9,... | collective-permute-start | bytes 1769480 | tf_op jit(solution)/shard_map/ppermute | solution.py:262
  8.4 19.2 %collective-permute-start.5 = (bf16[256,1152]{1,0:T(8,128)(2,1)}, bf16[256,1152]{1,0:T(8,128)(2,1)}, u32[]{:S(2)}, u32[]{:S(2)}) collective-permute-start(bf16[256,1152]{1,0:T(8,128)(2,1)} %constant_dynamic-slice_fusion.12), channel_id=1, source_target_pairs={{4,0},{8,4},{12,8},{16,12},{20,16},{24,20},{28,24},{5,1},{9,5},{13... | collective-permute-start | bytes 1769480 | tf_op jit(solution)/shard_map/ppermute | solution.py:262
  13.7 5.9 %collective-permute-start = (bf16[1,16,1728]{2,1,0:T(8,128)(2,1)S(1)}, bf16[1,16,1728]{2,1,0:T(8,128)(2,1)S(1)}, u32[]{:S(2)}, u32[]{:S(2)}) collective-permute-start(bf16[1,16,1728]{2,1,0:T(8,128)(2,1)S(1)} %bitcast.511), channel_id=1, source_target_pairs={{0,2},{1,3},{2,0},{3,1},{4,6},{5,7},{6,4},{7,5},{8,10},{9,11},{10,... | collective-permute-start | bytes 165896 | tf_op jit(solution)/shard_map/ppermute | solution.py:257
  17.6 112.3 %copy-start.74 = (s32[16]{0:T(128)}, s32[16]{0:T(128)S(1)}, u32[]{:S(2)}) copy-start(s32[16]{0:T(128)S(1)} %get-tuple-element.117) | copy-start | bytes 196
  19.7 1.4 collective-permute-start.1
  27.6 48.6 %copy-start.4 = (bf16[1,288,1024]{2,1,0:T(8,128)(2,1)}, bf16[1,288,1024]{2,1,0:T(8,128)(2,1)S(1)}, u32[]{:S(2)}) copy-start(bf16[1,288,1024]{2,1,0:T(8,128)(2,1)S(1)} %get-tuple-element.133) | copy-start | bytes 1769476
  27.7 16.4 %collective-permute-start.6 = (bf16[256,1152]{1,0:T(8,128)(2,1)}, bf16[256,1152]{1,0:T(8,128)(2,1)S(1)}, u32[]{:S(2)}, u32[]{:S(2)}) collective-permute-start(bf16[256,1152]{1,0:T(8,128)(2,1)} %collective-permute-done.5), channel_id=1, source_target_pairs={{0,2},{1,3},{2,0},{3,1},{4,6},{5,7},{6,4},{7,5},{8,10},{9,11},{10,... | collective-permute-start | bytes 1769480 | tf_op jit(solution)/shard_map/ppermute | solution.py:257
  37.5 18.4 %collective-permute-start.3 = (bf16[256,1152]{1,0:T(8,128)(2,1)}, bf16[256,1152]{1,0:T(8,128)(2,1)S(1)}, u32[]{:S(2)}, u32[]{:S(2)}) collective-permute-start(bf16[256,1152]{1,0:T(8,128)(2,1)} %collective-permute-done.2), channel_id=1, source_target_pairs={{0,2},{1,3},{2,0},{3,1},{4,6},{5,7},{6,4},{7,5},{8,10},{9,11},{10,... | collective-permute-start | bytes 1769480 | tf_op jit(solution)/shard_map/ppermute | solution.py:257
  45.6 14.9 %collective-permute-start.7 = (bf16[2,256,1152]{2,1,0:T(8,128)(2,1)S(1)}, bf16[2,256,1152]{2,1,0:T(8,128)(2,1)S(1)}, u32[]{:S(2)}, u32[]{:S(2)}) collective-permute-start(bf16[2,256,1152]{2,1,0:T(8,128)(2,1)S(1)} %maximum_select_fusion.6), channel_id=1, source_target_pairs={{0,1},{1,0},{2,3},{3,2},{4,5},{5,4},{6,7},{7,6},{8,9},{9,8},{10,11... | collective-permute-start | bytes 3538952 | tf_op jit(solution)/shard_map/ppermute | solution.py:257
  57.4 4.2 collective-permute-start.4
  85.8 3.3 collective-permute-start.8
  93.2 15.9 %collective-permute-start.9 = (bf16[256,1152]{1,0:T(8,128)(2,1)}, bf16[256,1152]{1,0:T(8,128)(2,1)}, u32[]{:S(2)}, u32[]{:S(2)}) collective-permute-start(bf16[256,1152]{1,0:T(8,128)(2,1)} %fusion.89), channel_id=1, source_target_pairs={{0,2},{1,3},{2,0},{3,1},{4,6},{5,7},{6,4},{7,5},{8,10},{9,11},{10,... | collective-permute-start | bytes 1769480 | tf_op jit(solution)/shard_map/ppermute | solution.py:257
  112.9 15.1 %collective-permute-start.10 = (bf16[256,1152]{1,0:T(8,128)(2,1)}, bf16[256,1152]{1,0:T(8,128)(2,1)}, u32[]{:S(2)}, u32[]{:S(2)}) collective-permute-start(bf16[256,1152]{1,0:T(8,128)(2,1)} %fusion.70), channel_id=1, source_target_pairs={{0,2},{1,3},{2,0},{3,1},{4,6},{5,7},{6,4},{7,5},{8,10},{9,11},{10,... | collective-permute-start | bytes 1769480 | tf_op jit(solution)/shard_map/ppermute | solution.py:257
  129.9 7.1 %collective-permute-start.11 = (bf16[2,256,1152]{2,1,0:T(8,128)(2,1)S(1)}, bf16[2,256,1152]{2,1,0:T(8,128)(2,1)S(1)}, u32[]{:S(2)}, u32[]{:S(2)}) collective-permute-start(bf16[2,256,1152]{2,1,0:T(8,128)(2,1)S(1)} %maximum_select_fusion.8), channel_id=1, source_target_pairs={{0,1},{1,0},{2,3},{3,2},{4,5},{5,4},{6,7},{7,6},{8,9},{9,8},{10,11... | collective-permute-start | bytes 3538952 | tf_op jit(solution)/shard_map/ppermute | solution.py:257
  153.4 6.7 %collective-permute-start.12 = (bf16[2,256,1152]{2,1,0:T(8,128)(2,1)S(1)}, bf16[2,256,1152]{2,1,0:T(8,128)(2,1)S(1)}, u32[]{:S(2)}, u32[]{:S(2)}) collective-permute-start(bf16[2,256,1152]{2,1,0:T(8,128)(2,1)S(1)} %dynamic-slice_bitcast_fusion.4), channel_id=1, source_target_pairs={{0,1},{1,0},{2,3},{3,2},{4,5},{5,4},{6,7},{7,6},{8,9},{9,8},{10,11... | collective-permute-start | bytes 3538952 | tf_op jit(solution)/shard_map/ppermute | solution.py:257
  160.5 15.7 %collective-permute-start.13 = (bf16[256,1152]{1,0:T(8,128)(2,1)S(1)}, bf16[256,1152]{1,0:T(8,128)(2,1)S(1)}, u32[]{:S(2)}, u32[]{:S(2)}) collective-permute-start(bf16[256,1152]{1,0:T(8,128)(2,1)S(1)} %fusion.90), channel_id=1, source_target_pairs={{0,2},{1,3},{2,0},{3,1},{4,6},{5,7},{6,4},{7,5},{8,10},{9,11},{10,... | collective-permute-start | bytes 1769480 | tf_op jit(solution)/shard_map/ppermute | solution.py:257
  182.8 15.3 %collective-permute-start.14 = (bf16[256,1152]{1,0:T(8,128)(2,1)S(1)}, bf16[256,1152]{1,0:T(8,128)(2,1)S(1)}, u32[]{:S(2)}, u32[]{:S(2)}) collective-permute-start(bf16[256,1152]{1,0:T(8,128)(2,1)S(1)} %get-tuple-element.111), channel_id=1, source_target_pairs={{0,2},{1,3},{2,0},{3,1},{4,6},{5,7},{6,4},{7,5},{8,10},{9,11},{10,... | collective-permute-start | bytes 1769480 | tf_op jit(solution)/shard_map/ppermute | solution.py:257
  188.5 37.5 %collective-permute-start.42 = (bf16[2,2,144,1152]{3,2,1,0:T(8,128)(2,1)}, bf16[2,2,144,1152]{3,2,1,0:T(8,128)(2,1)S(1)}, u32[]{:S(2)}, u32[]{:S(2)}) collective-permute-start(bf16[2,2,144,1152]{3,2,1,0:T(8,128)(2,1)} %dynamic-slice_bitcast_fusion.1), channel_id=1, source_target_pairs={{0,4},{4,0},{8,12},{12,8},{16,20},{20,16},{24,28},{28,24},{1,5},{5... | collective-permute-start | bytes 3981320 | tf_op jit(solution)/shard_map/ppermute | solution.py:257
  195.4 71.7 %collective-permute-start.39 = (bf16[2,2,144,1152]{3,2,1,0:T(8,128)(2,1)}, bf16[2,2,144,1152]{3,2,1,0:T(8,128)(2,1)S(1)}, u32[]{:S(2)}, u32[]{:S(2)}) collective-permute-start(bf16[2,2,144,1152]{3,2,1,0:T(8,128)(2,1)} %dynamic-slice_bitcast_fusion), channel_id=1, source_target_pairs={{0,4},{4,0},{8,12},{12,8},{16,20},{20,16},{24,28},{28,24},{1,5},{5... | collective-permute-start | bytes 3981320 | tf_op jit(solution)/shard_map/ppermute | solution.py:257
  198.3 6.2 %collective-permute-start.15 = (bf16[2,256,1152]{2,1,0:T(8,128)(2,1)S(1)}, bf16[2,256,1152]{2,1,0:T(8,128)(2,1)S(1)}, u32[]{:S(2)}, u32[]{:S(2)}) collective-permute-start(bf16[2,256,1152]{2,1,0:T(8,128)(2,1)S(1)} %maximum_select_fusion.10), channel_id=1, source_target_pairs={{0,1},{1,0},{2,3},{3,2},{4,5},{5,4},{6,7},{7,6},{8,9},{9,8},{10,11... | collective-permute-start | bytes 3538952 | tf_op jit(solution)/shard_map/ppermute | solution.py:257
  203.7 23.5 %collective-permute-start.16 = (bf16[2,256,1152]{2,1,0:T(8,128)(2,1)S(1)}, bf16[2,256,1152]{2,1,0:T(8,128)(2,1)S(1)}, u32[]{:S(2)}, u32[]{:S(2)}) collective-permute-start(bf16[2,256,1152]{2,1,0:T(8,128)(2,1)S(1)} %dynamic-slice_bitcast_fusion.3), channel_id=1, source_target_pairs={{0,1},{1,0},{2,3},{3,2},{4,5},{5,4},{6,7},{7,6},{8,9},{9,8},{10,11... | collective-permute-start | bytes 3538952 | tf_op jit(solution)/shard_map/ppermute | solution.py:257
  207.6 80.4 %collective-permute-start.21 = (f32[2,4,1,1024]{3,2,1,0:T(1,128)S(1)}, f32[2,4,1,1024]{3,2,1,0:T(1,128)S(1)}, u32[]{:S(2)}, u32[]{:S(2)}) collective-permute-start(f32[2,4,1,1024]{3,2,1,0:T(1,128)S(1)} %pad_maximum_fusion.8), channel_id=1, source_target_pairs={{4,0},{8,4},{12,8},{16,12},{20,16},{24,20},{28,24},{5,1},{9,5},{13... | collective-permute-start | bytes 98312 | tf_op jit(solution)/shard_map/ppermute | solution.py:262
  209.1 85.5 %collective-permute-start.20 = (f32[2,4,1,1024]{3,2,1,0:T(1,128)S(1)}, f32[2,4,1,1024]{3,2,1,0:T(1,128)S(1)}, u32[]{:S(2)}, u32[]{:S(2)}) collective-permute-start(f32[2,4,1,1024]{3,2,1,0:T(1,128)S(1)} %pad_maximum_fusion.8), channel_id=1, source_target_pairs={{0,4},{4,8},{8,12},{12,16},{16,20},{20,24},{24,28},{1,5},{5,9},{9,... | collective-permute-start | bytes 98312 | tf_op jit(solution)/shard_map/ppermute | solution.py:262
  226.0 72.8 %collective-permute-start.19 = (bf16[4,72,1024]{2,1,0:T(8,128)(2,1)S(1)}, bf16[4,72,1024]{2,1,0:T(8,128)(2,1)}, u32[]{:S(2)}, u32[]{:S(2)}) collective-permute-start(bf16[4,72,1024]{2,1,0:T(8,128)(2,1)S(1)} %bitcast.460), channel_id=1, source_target_pairs={{4,0},{8,4},{12,8},{16,12},{20,16},{24,20},{28,24},{5,1},{9,5},{13... | collective-permute-start | bytes 1769480 | tf_op jit(solution)/shard_map/ppermute | solution.py:262
  227.3 71.5 %collective-permute-start.18 = (bf16[4,72,1024]{2,1,0:T(8,128)(2,1)S(1)}, bf16[4,72,1024]{2,1,0:T(8,128)(2,1)}, u32[]{:S(2)}, u32[]{:S(2)}) collective-permute-start(bf16[4,72,1024]{2,1,0:T(8,128)(2,1)S(1)} %bitcast.461), channel_id=1, source_target_pairs={{0,4},{4,8},{8,12},{12,16},{16,20},{20,24},{24,28},{1,5},{5,9},{9,... | collective-permute-start | bytes 1769480 | tf_op jit(solution)/shard_map/ppermute | solution.py:262
  267.0 27.7 %collective-permute-start.17 = (bf16[256,1152]{1,0:T(8,128)(2,1)}, bf16[256,1152]{1,0:T(8,128)(2,1)}, u32[]{:S(2)}, u32[]{:S(2)}) collective-permute-start(bf16[256,1152]{1,0:T(8,128)(2,1)} %fusion.91), channel_id=1, source_target_pairs={{0,2},{1,3},{2,0},{3,1},{4,6},{5,7},{6,4},{7,5},{8,10},{9,11},{10,... | collective-permute-start | bytes 1769480 | tf_op jit(solution)/shard_map/ppermute | solution.py:257
  288.0 51.8 %collective-permute-start.43 = (bf16[2,144,1152]{2,1,0:T(8,128)(2,1)}, bf16[2,144,1152]{2,1,0:T(8,128)(2,1)}, u32[]{:S(2)}, u32[]{:S(2)}) collective-permute-start(bf16[2,144,1152]{2,1,0:T(8,128)(2,1)} %fusion.88), channel_id=1, source_target_pairs={{0,16},{4,20},{8,24},{12,28},{16,0},{20,4},{24,8},{28,12},{1,17},{... | collective-permute-start | bytes 1990664 | tf_op jit(solution)/shard_map/ppermute | solution.py:257
  294.6 73.6 %collective-permute-start.40 = (bf16[2,144,1152]{2,1,0:T(8,128)(2,1)}, bf16[2,144,1152]{2,1,0:T(8,128)(2,1)}, u32[]{:S(2)}, u32[]{:S(2)}) collective-permute-start(bf16[2,144,1152]{2,1,0:T(8,128)(2,1)} %fusion.87), channel_id=1, source_target_pairs={{0,16},{4,20},{8,24},{12,28},{16,0},{20,4},{24,8},{28,12},{1,17},{... | collective-permute-start | bytes 1990664 | tf_op jit(solution)/shard_map/ppermute | solution.py:257
  294.8 45.9 %collective-permute-start.34 = (bf16[2,2,144,576]{3,2,1,0:T(8,128)(2,1)}, bf16[2,2,144,576]{3,2,1,0:T(8,128)(2,1)}, u32[]{:S(2)}, u32[]{:S(2)}) collective-permute-start(bf16[2,2,144,576]{3,2,1,0:T(8,128)(2,1)} %fusion.79), channel_id=1, source_target_pairs={{0,4},{4,0},{8,12},{12,8},{16,20},{20,16},{24,28},{28,24},{1,5},{5... | collective-permute-start | bytes 1990664 | tf_op jit(solution)/shard_map/ppermute | solution.py:257
  311.1 61.2 %collective-permute-start.28 = (bf16[2,2,144,576]{3,2,1,0:T(8,128)(2,1)}, bf16[2,2,144,576]{3,2,1,0:T(8,128)(2,1)}, u32[]{:S(2)}, u32[]{:S(2)}) collective-permute-start(bf16[2,2,144,576]{3,2,1,0:T(8,128)(2,1)} %fusion.85), channel_id=1, source_target_pairs={{0,4},{4,0},{8,12},{12,8},{16,20},{20,16},{24,28},{28,24},{1,5},{5... | collective-permute-start | bytes 1990664 | tf_op jit(solution)/shard_map/ppermute | solution.py:257
  338.5 7.5 %collective-permute-start.24 = (f32[28800]{0:T(1024)S(1)}, f32[28800]{0:T(1024)S(1)}, u32[]{:S(2)}, u32[]{:S(2)}) collective-permute-start(f32[28800]{0:T(1024)S(1)} %get-tuple-element.153), channel_id=1, source_target_pairs={{0,3},{1,2},{2,1},{3,0},{4,7},{5,6},{6,5},{7,4},{8,11},{9,10},{10,... | collective-permute-start | bytes 345608 | tf_op jit(solution)/shard_map/ppermute | solution.py:257
  339.7 6.6 %collective-permute-start.22 = (f32[28800]{0:T(1024)S(1)}, f32[28800]{0:T(1024)S(1)}, u32[]{:S(2)}, u32[]{:S(2)}) collective-permute-start(f32[28800]{0:T(1024)S(1)} %get-tuple-element.154), channel_id=1, source_target_pairs={{0,1},{1,0},{2,3},{3,2},{4,5},{5,4},{6,7},{7,6},{8,9},{9,8},{10,11... | collective-permute-start | bytes 345608 | tf_op jit(solution)/shard_map/ppermute | solution.py:257
  340.7 9.1 %collective-permute-start.23 = (f32[28800]{0:T(1024)S(1)}, f32[28800]{0:T(1024)S(1)}, u32[]{:S(2)}, u32[]{:S(2)}) collective-permute-start(f32[28800]{0:T(1024)S(1)} %get-tuple-element.155), channel_id=1, source_target_pairs={{0,2},{1,3},{2,0},{3,1},{4,6},{5,7},{6,4},{7,5},{8,10},{9,11},{10,... | collective-permute-start | bytes 345608 | tf_op jit(solution)/shard_map/ppermute | solution.py:257
  346.3 16.7 %collective-permute-start.25 = (bf16[2,288,1024]{2,1,0:T(8,128)(2,1)}, bf16[2,288,1024]{2,1,0:T(8,128)(2,1)}, u32[]{:S(2)}, u32[]{:S(2)}) collective-permute-start(bf16[2,288,1024]{2,1,0:T(8,128)(2,1)} %dynamic-slice_bitcast_fusion.2), channel_id=1, source_target_pairs={{0,1},{1,0},{2,3},{3,2},{4,5},{5,4},{6,7},{7,6},{8,9},{9,8},{10,11... | collective-permute-start | bytes 3538952 | tf_op jit(solution)/shard_map/ppermute | solution.py:257
  346.3 13.9 %collective-permute-start.44 = (bf16[144,1152]{1,0:T(8,128)(2,1)S(1)}, bf16[144,1152]{1,0:T(8,128)(2,1)}, u32[]{:S(2)}, u32[]{:S(2)}) collective-permute-start(bf16[144,1152]{1,0:T(8,128)(2,1)S(1)} %fusion.96), channel_id=1, source_target_pairs={{0,8},{4,12},{8,0},{12,4},{16,24},{20,28},{24,16},{28,20},{1,9},{5... | collective-permute-start | bytes 995336 | tf_op jit(solution)/shard_map/ppermute | solution.py:257
  349.7 42.2 %collective-permute-start.35 = (bf16[2,144,576]{2,1,0:T(8,128)(2,1)}, bf16[2,144,576]{2,1,0:T(8,128)(2,1)}, u32[]{:S(2)}, u32[]{:S(2)}) collective-permute-start(bf16[2,144,576]{2,1,0:T(8,128)(2,1)} %fusion.94), channel_id=1, source_target_pairs={{0,16},{4,20},{8,24},{12,28},{16,0},{20,4},{24,8},{28,12},{1,17},{... | collective-permute-start | bytes 995336 | tf_op jit(solution)/shard_map/ppermute | solution.py:257
  360.2 6.3 %collective-permute-start.26 = (f32[31680]{0:T(1024)S(1)}, f32[31680]{0:T(1024)S(1)}, u32[]{:S(2)}, u32[]{:S(2)}) collective-permute-start(f32[31680]{0:T(1024)S(1)} %concatenate.159), channel_id=1, source_target_pairs={{0,4},{4,0},{8,12},{12,8},{16,20},{20,16},{24,28},{28,24},{1,5},{5... | collective-permute-start | bytes 380168 | tf_op jit(solution)/shard_map/ppermute | solution.py:257
  365.7 50.1 %collective-permute-start.30 = (bf16[288,1024]{1,0:T(8,128)(2,1)}, bf16[288,1024]{1,0:T(8,128)(2,1)}, u32[]{:S(2)}, u32[]{:S(2)}) collective-permute-start(bf16[288,1024]{1,0:T(8,128)(2,1)} %fusion.92), channel_id=1, source_target_pairs={{0,2},{1,3},{2,0},{3,1},{4,6},{5,7},{6,4},{7,5},{8,10},{9,11},{10,... | collective-permute-start | bytes 1769480 | tf_op jit(solution)/shard_map/ppermute | solution.py:257
  366.6 5.7 %collective-permute-start.27 = (f32[31680]{0:T(1024)S(1)}, f32[31680]{0:T(1024)S(1)}, u32[]{:S(2)}, u32[]{:S(2)}) collective-permute-start(f32[31680]{0:T(1024)S(1)} %add.754), channel_id=1, source_target_pairs={{0,8},{4,12},{8,0},{12,4},{16,24},{20,28},{24,16},{28,20},{1,9},{5... | collective-permute-start | bytes 380168 | tf_op jit(solution)/shard_map/ppermute | solution.py:257
  374.5 10.2 %collective-permute-start.29 = (f32[31680]{0:T(1024)S(1)}, f32[31680]{0:T(1024)S(1)}, u32[]{:S(2)}, u32[]{:S(2)}) collective-permute-start(f32[31680]{0:T(1024)S(1)} %add.755), channel_id=1, source_target_pairs={{0,16},{4,20},{8,24},{12,28},{16,0},{20,4},{24,8},{28,12},{1,17},{... | collective-permute-start | bytes 380168 | tf_op jit(solution)/shard_map/ppermute | solution.py:257
  380.3 20.5 %collective-permute-start.41 = (bf16[144,1152]{1,0:T(8,128)(2,1)}, bf16[144,1152]{1,0:T(8,128)(2,1)}, u32[]{:S(2)}, u32[]{:S(2)}) collective-permute-start(bf16[144,1152]{1,0:T(8,128)(2,1)} %fusion.95), channel_id=1, source_target_pairs={{0,8},{4,12},{8,0},{12,4},{16,24},{20,28},{24,16},{28,20},{1,9},{5... | collective-permute-start | bytes 995336 | tf_op jit(solution)/shard_map/ppermute | solution.py:257
  388.5 7.2 %collective-permute-start.31 = (f32[2,288]{1,0:T(2,128)S(1)}, f32[2,288]{1,0:T(2,128)S(1)}, u32[]{:S(2)}, u32[]{:S(2)}) collective-permute-start(f32[2,288]{1,0:T(2,128)S(1)} %bitcast.534), channel_id=1, source_target_pairs={{0,1},{1,0},{2,3},{3,2},{4,5},{5,4},{6,7},{7,6},{8,9},{9,8},{10,11... | collective-permute-start | bytes 6920 | tf_op jit(solution)/shard_map/ppermute | solution.py:257
  388.6 8.9 %collective-permute-start.32 = (f32[2,288]{1,0:T(2,128)S(1)}, f32[2,288]{1,0:T(2,128)S(1)}, u32[]{:S(2)}, u32[]{:S(2)}) collective-permute-start(f32[2,288]{1,0:T(2,128)S(1)} %bitcast.533), channel_id=1, source_target_pairs={{0,2},{1,3},{2,0},{3,1},{4,6},{5,7},{6,4},{7,5},{8,10},{9,11},{10,... | collective-permute-start | bytes 6920 | tf_op jit(solution)/shard_map/ppermute | solution.py:257
  391.9 8.2 %collective-permute-start.33 = (f32[2,288]{1,0:T(2,128)S(1)}, f32[2,288]{1,0:T(2,128)S(1)}, u32[]{:S(2)}, u32[]{:S(2)}) collective-permute-start(f32[2,288]{1,0:T(2,128)S(1)} %bitcast.532), channel_id=1, source_target_pairs={{0,3},{1,2},{2,1},{3,0},{4,7},{5,6},{6,5},{7,4},{8,11},{9,10},{10,... | collective-permute-start | bytes 6920 | tf_op jit(solution)/shard_map/ppermute | solution.py:257
  395.8 19.8 %collective-permute-start.37 = (bf16[2,144,576]{2,1,0:T(8,128)(2,1)}, bf16[2,144,576]{2,1,0:T(8,128)(2,1)S(1)}, u32[]{:S(2)}, u32[]{:S(2)}) collective-permute-start(bf16[2,144,576]{2,1,0:T(8,128)(2,1)} %fusion.93), channel_id=1, source_target_pairs={{0,16},{4,20},{8,24},{12,28},{16,0},{20,4},{24,8},{28,12},{1,17},{... | collective-permute-start | bytes 995336 | tf_op jit(solution)/shard_map/ppermute | solution.py:257
  397.5 12.6 %collective-permute-start.36 = (bf16[144,576]{1,0:T(8,128)(2,1)S(1)}, bf16[144,576]{1,0:T(8,128)(2,1)S(1)}, u32[]{:S(2)}, u32[]{:S(2)}) collective-permute-start(bf16[144,576]{1,0:T(8,128)(2,1)S(1)} %fusion.97), channel_id=1, source_target_pairs={{0,8},{4,12},{8,0},{12,4},{16,24},{20,28},{24,16},{28,20},{1,9},{5... | collective-permute-start | bytes 497672 | tf_op jit(solution)/shard_map/ppermute | solution.py:257
  415.7 6.1 %collective-permute-start.38 = (bf16[144,576]{1,0:T(8,128)(2,1)S(1)}, bf16[144,576]{1,0:T(8,128)(2,1)S(1)}, u32[]{:S(2)}, u32[]{:S(2)}) collective-permute-start(bf16[144,576]{1,0:T(8,128)(2,1)S(1)} %fusion.98), channel_id=1, source_target_pairs={{0,8},{4,12},{8,0},{12,4},{16,24},{20,28},{24,16},{28,20},{1,9},{5... | collective-permute-start | bytes 497672 | tf_op jit(solution)/shard_map/ppermute | solution.py:257
  (102 other events, 710.7 us)
